TPU v7x, 512 devices: a whole 4x8x8 slice. The times are simulated.
512 devices in a mesh: dp: 32 (over x, z), expert: 16 (over y, core).
Axes of the slice: x: 4, y: 8, z: 8, core: 2. Of those that a mesh axis runs over, the one named last changes fastest.
Arguments:
- xin: bfloat16 [2, 4096, 8192], P(None, 'dp', 'expert'), may hold values from -6 to 6
- zin: bfloat16 [2, 4096, 8192], P(None, 'dp', 'expert'), may hold values from -6 to 6
- cotangent: bfloat16 [2, 4096, 8192], P(None, 'dp', 'expert'), may hold values from -6 to 6
- conv_weight: float32 [4, 8192], P(None, 'expert'), may hold values from -3 to 3
- conv_bias: float32 [8192], P('expert'), may hold values from -3 to 3
- proj_weight: bfloat16 [288, 8192], P('dp', 'expert'), may hold values from -0.0625 to 0.0625
- dt_weight: bfloat16 [256, 8192], P('dp', 'expert'), may hold values from -0.375 to 0.375
- dt_bias: float32 [8192], P('expert'), may hold values from -5 to -1
- a_log: float32 [16, 8192], P(None, 'expert'), may hold values from -8 to 2
- d_skip: float32 [8192], P('expert'), may hold values from 0.5 to 1.5
Outputs:
- grad_x: bfloat16 [2, 4096, 8192], P(None, 'dp', 'expert')
- grad_gate: bfloat16 [2, 4096, 8192], P(None, 'dp', 'expert')
- grad_proj_weight: float32 [256, 8192], P('dp', 'expert')
- grad_state_weight: float32 [32, 8192], P(None, 'expert')
- grad_dt_weight: float32 [256, 8192], P('dp', 'expert')
- grad_conv_weight: float32 [4, 8192], P(None, 'expert')
- grad_conv_bias: float32 [8192], P('expert')
- grad_dt_bias: float32 [8192], P('expert')
- grad_a_log: float32 [16, 8192], P(None, 'expert')
- grad_d_skip: float32 [8192], P('expert')
All inputs are finite; a program needn't handle non-finite values.
Results may differ from a plain program's by a relative error of at most 0.007.
Values may be sent and summed in bfloat16 or wider, within the bound.
A program may use at most 64 MiB of HBM per device.

v0:
```python
import jax
import jax.numpy as jnp
from jax import lax
from jax.sharding import PartitionSpec as P

unroll_steps = 8


def shifted(block, axis, distance):
    devices = range(lax.axis_size(axis))
    route = [(i - distance, i) for i in devices if i - distance in devices]
    return lax.ppermute(block, axis, route)


def prefix(part, axis, combine, identity, reverse):
    count = lax.axis_size(axis)
    place = lax.axis_index(axis)
    ahead = count - 1 - place if reverse else place
    gathered = jax.tree.map(lambda a: lax.all_gather(a, axis), part)
    state = jax.tree.map(lambda a, e: jnp.zeros_like(a) + jnp.asarray(e, a.dtype), part, identity)

    def one(lap, state):
        source = count - 1 - lap if reverse else lap
        return combine(
            state, jax.tree.map(lambda a: lax.dynamic_index_in_dim(a, source, 0, False), gathered)
        )

    return lax.fori_loop(0, ahead, one, state)


def contract_last(left_side, right_side):
    return lax.dot_general(
        left_side, right_side, (((1,), (1,)), ((), ())), preferred_element_type=jnp.float32
    )


def contract_first(left_side, right_side):
    return lax.dot_general(
        left_side, right_side, (((0,), (0,)), ((), ())), preferred_element_type=jnp.float32
    )


def linear_combine(earlier, later_part):
    return (earlier[0] * later_part[0], later_part[0] * earlier[1] + later_part[1])


def advance(decay_rate, carried, step_now, x_now, b_now):
    decay_now = jnp.exp(step_now[:, None, :] * decay_rate[None])
    return (decay_now, decay_now * carried + b_now[:, :, None] * (step_now * x_now)[:, None, :])


def slice_rows(arrays, first_row):
    return [lax.dynamic_slice_in_dim(values, first_row, unroll_steps, 1) for values in arrays]


def run_forward(decay_rate, step_size, x_value, b_matrix, c_matrix, begin_state, with_output):
    turn_count = step_size.shape[1] // unroll_steps

    def one_turn(carried, counter):
        step_part, x_part, b_part, c_part = slice_rows(
            (step_size, x_value, b_matrix, c_matrix), counter * unroll_steps
        )
        checkpoint = carried
        outputs = []
        for offset in range(unroll_steps):
            unused, carried = advance(
                decay_rate, carried, step_part[:, offset], x_part[:, offset], b_part[:, offset]
            )
            if with_output:
                outputs.append(jnp.sum(c_part[:, offset, :, None] * carried, axis=1))
        if with_output:
            return (carried, (checkpoint, jnp.stack(outputs, 1)))
        return (carried, None)

    return lax.scan(one_turn, begin_state, jnp.arange(turn_count, dtype=jnp.int32))


def adjoint_start(decay_rate, step_size, c_matrix, grad_y):
    seq_count, block_len, channels = step_size.shape
    turn_count = block_len // unroll_steps

    def one_turn(passed, counter):
        step_part, c_part, gy_part = slice_rows(
            (step_size, c_matrix, grad_y), counter * unroll_steps
        )
        for offset in reversed(range(unroll_steps)):
            decay_now = jnp.exp(step_part[:, offset, None, :] * decay_rate[None])
            passed = decay_now * (c_part[:, offset, :, None] * gy_part[:, offset, None, :] + passed)
        return (passed, None)

    zero_state = jnp.zeros((seq_count, decay_rate.shape[0], channels), jnp.float32)
    passed, unused = lax.scan(
        one_turn, zero_state, jnp.arange(turn_count, dtype=jnp.int32), reverse=True
    )
    return passed


def run_adjoint(decay_rate, step_size, x_value, b_matrix, c_matrix, grad_y, checkpoints, incoming):
    seq_count, block_len, channels = step_size.shape
    turn_count = block_len // unroll_steps

    def one_turn(carried, pieces):
        passed, decay_grad = carried
        counter, begin_state = pieces
        step_part, x_part, b_part, c_part, gy_part = slice_rows(
            (step_size, x_value, b_matrix, c_matrix, grad_y), counter * unroll_steps
        )
        history = [begin_state]
        decays = []
        for offset in range(unroll_steps):
            decay_now, next_state = advance(
                decay_rate, history[-1], step_part[:, offset], x_part[:, offset], b_part[:, offset]
            )
            decays.append(decay_now)
            history.append(next_state)
        results = [None] * unroll_steps
        for offset in reversed(range(unroll_steps)):
            step_now = step_part[:, offset]
            x_now = x_part[:, offset]
            adjoint = c_part[:, offset, :, None] * gy_part[:, offset, None, :] + passed
            grad_c = jnp.sum(gy_part[:, offset, None, :] * history[offset + 1], axis=2)
            grad_b = jnp.sum(adjoint * (step_now * x_now)[:, None, :], axis=2)
            b_adjoint = jnp.sum(b_part[:, offset, :, None] * adjoint, axis=1)
            prev_term = adjoint * history[offset] * decays[offset]
            grad_step = x_now * b_adjoint + jnp.sum(prev_term * decay_rate[None], axis=1)
            decay_grad = decay_grad + prev_term * step_now[:, None, :]
            passed = decays[offset] * adjoint
            results[offset] = (grad_c, grad_b, step_now * b_adjoint, grad_step)
        stacked = tuple(
            (jnp.stack([member[column] for member in results], 1) for column in range(4))
        )
        return ((passed, decay_grad), stacked)

    zero_grad = jnp.zeros(incoming.shape, jnp.float32)
    (passed, decay_grad), stacked = lax.scan(
        one_turn,
        (incoming, zero_grad),
        (jnp.arange(turn_count, dtype=jnp.int32), checkpoints),
        reverse=True,
    )
    unfolded = [jnp.moveaxis(member, 0, 1).reshape(seq_count, block_len, -1) for member in stacked]
    return (jnp.sum(decay_grad, axis=0), unfolded)


def body(
    xin, zin, cotangent, conv_weight, conv_bias, proj_weight, dt_weight, dt_bias, a_log, d_skip
):
    seq_count, block_len, channels = xin.shape
    kernel_len = conv_weight.shape[0]
    state_count = a_log.shape[0]
    row_count = seq_count * block_len
    x_input = xin.astype(jnp.float32)
    front_rows = shifted(xin[:, block_len - (kernel_len - 1) :, :], "dp", 1)
    padded = jnp.concatenate([front_rows.astype(jnp.float32), x_input], 1)
    preact = conv_bias[None, None, :] + jnp.zeros_like(x_input)
    for tap_index in range(kernel_len):
        preact = (
            preact
            + conv_weight[tap_index][None, None, :] * padded[:, tap_index : tap_index + block_len]
        )
    pre_sig = jax.nn.sigmoid(preact)
    x_conv = (preact * pre_sig).astype(jnp.bfloat16)
    x_flat = x_conv.reshape(row_count, channels)
    x_value = x_conv.astype(jnp.float32)
    proj_full, dt_full = (
        lax.all_gather(proj_weight, "dp", axis=0, tiled=True),
        lax.all_gather(dt_weight, "dp", axis=0, tiled=True),
    )
    low_rank = dt_full.shape[0]
    projected = lax.psum(contract_last(x_flat, proj_full), "expert")
    dt_low = projected[:, :low_rank].astype(jnp.bfloat16)
    b_matrix = projected[:, low_rank : low_rank + state_count].reshape(
        seq_count, block_len, state_count
    )
    c_matrix = projected[:, low_rank + state_count :].reshape(seq_count, block_len, state_count)
    dt_pre = jnp.dot(dt_low, dt_full, preferred_element_type=jnp.float32) + dt_bias[None, :]
    step_size = jax.nn.softplus(dt_pre).reshape(seq_count, block_len, channels)
    decay_rate = -jnp.exp(a_log)
    zero_state = jnp.zeros((seq_count, state_count, channels), jnp.float32)
    local_end, unused = run_forward(
        decay_rate, step_size, x_value, b_matrix, c_matrix, zero_state, False
    )
    total_decay = jnp.exp(decay_rate[None] * jnp.sum(step_size, axis=1)[:, None, :])
    identity = (jnp.ones_like(total_decay), jnp.zeros_like(local_end))
    unused_decay, incoming = prefix((total_decay, local_end), "dp", linear_combine, identity, False)
    unused_end, (checkpoints, scan_out) = run_forward(
        decay_rate, step_size, x_value, b_matrix, c_matrix, incoming, True
    )
    y_value = (
        jnp.moveaxis(scan_out, 0, 1).reshape(seq_count, block_len, channels)
        + d_skip[None, None, :] * x_value
    )
    z_value = zin.astype(jnp.float32)
    g_value = cotangent.astype(jnp.float32)
    z_sig = jax.nn.sigmoid(z_value)
    grad_gate = (g_value * y_value * z_sig * (1.0 + z_value * (1.0 - z_sig))).astype(jnp.bfloat16)
    grad_y = g_value * z_value * z_sig
    local_passed = adjoint_start(decay_rate, step_size, c_matrix, grad_y)
    unused_back, later_adjoint = prefix(
        (total_decay, local_passed), "dp", linear_combine, identity, True
    )
    decay_total, (grad_c, grad_b, grad_scan_x, grad_step) = run_adjoint(
        decay_rate, step_size, x_value, b_matrix, c_matrix, grad_y, checkpoints, later_adjoint
    )
    grad_dt_pre = grad_step.reshape(row_count, channels) * jax.nn.sigmoid(dt_pre)
    grad_dt_round = grad_dt_pre.astype(jnp.bfloat16)
    grad_partial = jnp.concatenate(
        [
            contract_last(grad_dt_round, dt_full),
            grad_b.reshape(row_count, state_count),
            grad_c.reshape(row_count, state_count),
        ],
        1,
    )
    grad_projected = lax.psum(grad_partial, "expert").astype(jnp.bfloat16)
    proj_terms = contract_first(grad_projected, x_flat)
    grad_proj_weight, grad_dt_weight = (
        lax.psum_scatter(proj_terms[:low_rank], "dp", scatter_dimension=0, tiled=True),
        lax.psum_scatter(
            contract_first(dt_low, grad_dt_round), "dp", scatter_dimension=0, tiled=True
        ),
    )
    grad_conv_x = (
        d_skip[None, None, :] * grad_y
        + grad_scan_x
        + jnp.dot(grad_projected, proj_full, preferred_element_type=jnp.float32).reshape(
            seq_count, block_len, channels
        )
    )
    grad_preact = grad_conv_x * pre_sig * (1.0 + preact * (1.0 - pre_sig))
    after_rows = shifted(grad_preact[:, : kernel_len - 1, :], "dp", -1)
    grad_padded = jnp.concatenate([grad_preact, after_rows], 1)
    grad_input = jnp.zeros_like(grad_preact)
    for tap_index in range(kernel_len):
        shift_by = kernel_len - 1 - tap_index
        grad_input = (
            grad_input
            + conv_weight[tap_index][None, None, :]
            * grad_padded[:, shift_by : shift_by + block_len]
        )
    conv_terms = jnp.stack(
        [
            jnp.sum(grad_preact * padded[:, tap_index : tap_index + block_len], axis=(0, 1))
            for tap_index in range(kernel_len)
        ],
        0,
    )
    grad_state_weight, grad_conv_weight, grad_conv_bias, grad_dt_bias, decay_sum, grad_d_skip = (
        lax.psum(
            (
                proj_terms[low_rank:],
                conv_terms,
                jnp.sum(grad_preact, axis=(0, 1)),
                jnp.sum(grad_dt_pre, axis=0),
                decay_total,
                jnp.sum(grad_y * x_value, axis=(0, 1)),
            ),
            "dp",
        )
    )
    grad_a_log = decay_sum * decay_rate
    return (
        grad_input.astype(jnp.bfloat16),
        grad_gate,
        grad_proj_weight,
        grad_state_weight,
        grad_dt_weight,
        grad_conv_weight,
        grad_conv_bias,
        grad_dt_bias,
        grad_a_log,
        grad_d_skip,
    )


def solution(mesh):
    return jax.shard_map(
        body,
        mesh=mesh,
        in_specs=(
            P(None, "dp", "expert"),
            P(None, "dp", "expert"),
            P(None, "dp", "expert"),
            P(None, "expert"),
            P("expert"),
            P("dp", "expert"),
            P("dp", "expert"),
            P("expert"),
            P(None, "expert"),
            P("expert"),
        ),
        out_specs=(
            P(None, "dp", "expert"),
            P(None, "dp", "expert"),
            P("dp", "expert"),
            P(None, "expert"),
            P("dp", "expert"),
            P(None, "expert"),
            P("expert"),
            P("expert"),
            P(None, "expert"),
            P("expert"),
        ),
        check_vma=False,
    )
```

profile of v0, /device:TPU:1, one launch (start us, length us, event | category | flops | bytes accessed | tf_op | source)
XLA Modules:
  0.0 1566.3 jit_solution(7143931201976610156)
XLA Ops:
  8.0 4.8 collective-permute-start
  13.7 43.0 %all-gather.2 = bf16[32,9,512]{2,1,0:T(8,128)(2,1)S(1)} all-gather(bf16[1,9,512]{2,1,0:T(8,128)(2,1)} %bitcast.600), channel_id=1, replica_groups=mesh['dp'=32,'expert'=16] {'dp'}, dimensions={0}, use_global_device_ids=true | all-gather | bytes 304128 | tf_op jit(solution)/shard_map/all_gather | solution.py:166
  56.7 34.7 %all_gather.25 = bf16[256,512]{1,0:T(8,128)(2,1)S(1)} all-gather(bf16[8,512]{1,0:T(8,128)(2,1)} %param.28), channel_id=1, replica_groups=mesh['dp'=32,'expert'=16] {'dp'}, dimensions={0}, use_global_device_ids=true | all-gather | bytes 270336 | tf_op jit(solution)/shard_map/all_gather | solution.py:167
  92.7 1.9 multiply_reduce_fusion.40
  97.2 131.0 %all-reduce.5.cloned.1.call-done = f32[256,288]{0,1:T(8,128)} async-done(((f32[256,288]{0,1:T(8,128)}), f32[256,288]{0,1:T(8,128)}) %all-reduce.5.cloned.1.call-update) | async-done | bytes 294928 | tf_op jit(solution)/shard_map/psum | solution.py:170
  233.4 47.4 %while.94 = (s32[]{:T(128)}, f32[2,16,512]{2,1,0:T(8,128)S(1)}, s32[16]{0:T(128)S(1)}, f32[2,128,512]{2,0,1:T(2,128)S(1)}, f32[16,512]{1,0:T(8,128)S(1)}, /*inde...) while((s32[]{:T(128)}, f32[2,16,512]{2,1,0:T(8,128)S(1)}, ...), condition=%wide.region_3.4_spmd.clone, body=%wide.region_2.3_spmd.clone.sunk | while | flops 540687 | bytes 363929 | solution.py:92
  281.5 34.9 %while.95 = (s32[]{:T(128)}, f32[2,16,512]{2,1,0:T(8,128)S(1)}, s32[16]{0:T(128)S(1)}, f32[2,128,512]{2,0,1:T(2,128)S(1)}, f32[16,512]{1,0:T(8,128)S(1)}, /*inde...) while((s32[]{:T(128)}, f32[2,16,512]{2,1,0:T(8,128)S(1)}, ...), condition=%wide.region_7.8_spmd.clone, body=%wide.region_6.7_spmd.clone.sunk | while | flops 548878 | bytes 363909 | solution.py:75
  317.2 80.0 %all-gather.9.cloned.1.call-done = f32[64,16,512]{2,1,0:T(8,128)} async-done(((f32[2,16,512]{2,1,0:T(8,128)}), f32[64,16,512]{2,1,0:T(8,128)}) %all-gather.9.cloned.1.call-update) | async-done | bytes 2097168 | tf_op jit(solution)/shard_map/all_gather | solution.py:19
  397.2 28.7 %while.91 = (s32[]{:T(128)}, f32[2,16,512]{2,1,0:T(8,128)S(1)}, s32[]{:T(128)}, f32[32,2,16,512]{3,2,1,0:T(8,128)}, f32[32,2,16,512]{3,2,1,0:T(8,128)}, /*index=5*/s32[]{:T(128)}, s32[]{:T(128)}, s32[]{:T(128)}, s32[]{:T(128)}) while((s32[]{:T(128)}, f32[2,16,512]{2,1,0:T(8,128)S(1)}, s32[]{:T(128)}, f32[32,2,16,512]{3,2,1,0:T(8,128)}, ...), condition=%wide.region_5.6_spmd, body=%wide.region_4.5_spmd.sunk | while | flops 32774 | bytes 262295 | solution.py:28
  425.9 55.6 %all-gather.11.cloned.1.call-done = f32[64,16,512]{2,1,0:T(8,128)} async-done(((f32[2,16,512]{2,1,0:T(8,128)}), f32[64,16,512]{2,1,0:T(8,128)}) %all-gather.11.cloned.1.call-update) | async-done | bytes 2097168 | tf_op jit(solution)/shard_map/all_gather | solution.py:19
  481.5 63.3 %while.93 = (s32[]{:T(128)}, f32[2,16,512]{2,1,0:T(8,128)S(1)}, f32[16,2,16,512]{3,2,1,0:T(8,128)}, f32[16,2,8,512]{3,2,1,0:T(8,128)}, s32[16]{0:T(128)S(1)}, /*...) while((s32[]{:T(128)}, f32[2,16,512]{2,1,0:T(8,128)S(1)}, ...), condition=%wide.region_19.20_spmd, body=%wide.region_10.19_spmd.sunk | while | flops 1179661 | bytes 1039515 | solution.py:75
  548.8 337.0 %while.96 = (s32[]{:T(128)}, f32[2,16,512]{2,1,0:T(8,128)S(1)}, f32[2,16,512]{2,1,0:T(8,128)S(1)}, f32[16,2,8,16]{3,1,2,0:T(2,128)}, f32[16,2,8,16]{3,1,2,0:T(2,...) while((s32[]{:T(128)}, f32[2,16,512]{2,1,0:T(8,128)S(1)}, ...), condition=%wide.region_53.54_spmd.clone, body=%wide.region_20.53_spmd.clone.sunk | while | flops 5160461 | bytes 3020149 | solution.py:135
  556.0 1.6 multiply_reduce_fusion.61
  577.0 1.6 multiply_reduce_fusion.61
  598.1 1.6 multiply_reduce_fusion.61
  619.2 1.6 multiply_reduce_fusion.61
  640.2 1.6 multiply_reduce_fusion.61
  889.5 49.8 %all-reduce.8 = bf16[256,288]{0,1:T(8,128)(2,1)S(1)} all-reduce(f32[256,288]{0,1:T(8,128)S(1)} %pad_maximum_fusion.2), channel_id=1, replica_groups=mesh['dp'=32,'expert'=16] {'expert'}, use_global_device_ids=true, to_apply=%region_54.55 | all-reduce | flops 73728 | bytes 442368 | tf_op jit(solution)/shard_map/psum | solution.py:215
  941.2 2.0 fusion.190
  943.6 3.0 fusion.199
  948.0 141.3 %all-reduce = (f32[4,512]{1,0:T(4,128)}, f32[512]{0:T(512)}, f32[512]{0:T(512)}, f32[16,512]{1,0:T(8,128)S(1)}, f32[512]{0:T(512)}) all-reduce(f32[4,512]{1,0:T(4,128)S(1)} %pad_maximum_fusion.3, f32[512]{0:T(512)S(1)} %get-tuple-element.934, f32[512]{0:T(512)S(1)} %get-tuple-element.1053, ...), channel_id=1, replica_groups=mesh['dp'=32,'expert'=16] {'dp'}, use_global_device_ids=true, to_apply=%region_62.63 | all-reduce | flops 11776 | bytes 94208 | tf_op jit(solution)/shard_map/psum | solution.py:249
  1090.9 23.3 %all-reduce.7.cloned.1.call-done = f32[32,512]{1,0:T(8,128)} async-done(((f32[32,512]{1,0:T(8,128)}), f32[32,512]{1,0:T(8,128)}) %all-reduce.7.cloned.1.call-update) | async-done | bytes 65552 | tf_op jit(solution)/shard_map/psum | solution.py:249
  1114.2 221.5 %reduce-scatter.3.cloned.1.call-done = f32[8,512]{1,0:T(8,128)} async-done(((f32[256,512]{1,0:T(8,128)}), f32[8,512]{1,0:T(8,128)}) %reduce-scatter.3.cloned.1.call-update) | async-done | bytes 16400 | tf_op jit(solution)/shard_map/reduce_scatter | solution.py:218
  1335.8 222.2 %reduce-scatter.5.cloned.1.call-done = f32[8,512]{1,0:T(8,128)} async-done(((f32[256,512]{1,0:T(8,128)}), f32[8,512]{1,0:T(8,128)}) %reduce-scatter.5.cloned.1.call-update) | async-done | bytes 16400 | tf_op jit(solution)/shard_map/reduce_scatter | solution.py:219
  (1646 shorter events, 480.4 us)
Async XLA Ops:
  7.2 85.5 %copy-start.1 = (bf16[2,128,512]{2,1,0:T(8,128)(2,1)S(1)}, bf16[2,128,512]{2,1,0:T(8,128)(2,1)}, u32[]{:S(2)}) copy-start(bf16[2,128,512]{2,1,0:T(8,128)(2,1)} %param.23) | copy-start | bytes 786436
  7.2 85.5 %copy-start.2 = (bf16[2,128,512]{2,1,0:T(8,128)(2,1)S(1)}, bf16[2,128,512]{2,1,0:T(8,128)(2,1)}, u32[]{:S(2)}) copy-start(bf16[2,128,512]{2,1,0:T(8,128)(2,1)} %param.24) | copy-start | bytes 786436
  7.2 85.5 %copy-start.35 = (f32[512]{0:T(512)S(1)}, f32[512]{0:T(512)}, u32[]{:S(2)}) copy-start(f32[512]{0:T(512)} %param.26) | copy-start | bytes 6148
  7.2 221.0 %all-reduce.5.cloned.1.call-start = ((), (), s32[]{:S(2)}) async-start(), calls=%async_computation.2 | async-start | bytes 589824 | tf_op jit(solution)/shard_map/psum | solution.py:170
  8.0 84.6 %collective-permute-start = (bf16[2,3,512]{2,1,0:T(4,128)(2,1)S(1)}, bf16[2,3,512]{2,1,0:T(4,128)(2,1)S(1)}, u32[]{:S(2)}, u32[]{:S(2)}) collective-permute-start(bf16[2,3,512]{2,1,0:T(4,128)(2,1)S(1)} %slice.836), channel_id=1, source_target_pairs={{0,16},{16,32},{32,48},{48,64},{64,80},{80,96},{96,112},{112,128},... | collective-permute-start | bytes 18440 | tf_op jit(solution)/shard_map/ppermute | solution.py:12
  13.7 80.9 %copy-start.26 = (f32[1,512]{1,0:T(1,128)}, f32[1,512]{1,0:T(1,128)S(1)}, u32[]{:S(2)}) copy-start(f32[1,512]{1,0:T(1,128)S(1)} %get-tuple-element.1215) | copy-start | bytes 6148
  13.7 80.9 %copy-start.28 = (f32[1,512]{1,0:T(1,128)}, f32[1,512]{1,0:T(1,128)S(1)}, u32[]{:S(2)}) copy-start(f32[1,512]{1,0:T(1,128)S(1)} %get-tuple-element.1216) | copy-start | bytes 6148
  13.7 80.9 %copy-start.30 = (f32[1,512]{1,0:T(1,128)}, f32[1,512]{1,0:T(1,128)S(1)}, u32[]{:S(2)}) copy-start(f32[1,512]{1,0:T(1,128)S(1)} %get-tuple-element.1217) | copy-start | bytes 6148
  13.7 80.8 %copy-start.32 = (f32[1,512]{1,0:T(1,128)}, f32[1,512]{1,0:T(1,128)S(1)}, u32[]{:S(2)}) copy-start(f32[1,512]{1,0:T(1,128)S(1)} %get-tuple-element.1218) | copy-start | bytes 6148
  91.4 136.8 %copy-start.3 = (bf16[256,512]{1,0:T(8,128)(2,1)}, bf16[256,512]{1,0:T(8,128)(2,1)S(1)}, u32[]{:S(2)}) copy-start(bf16[256,512]{1,0:T(8,128)(2,1)S(1)} %all_gather.25) | copy-start | bytes 786436
  94.6 133.6 %copy-start.37 = (f32[512]{0:T(512)S(1)}, f32[512]{0:T(512)}, u32[]{:S(2)}) copy-start(f32[512]{0:T(512)} %param.29) | copy-start | bytes 6148
  95.6 221.5 %all-gather.7.cloned.1.call-start = ((), (), s32[]{:S(2)}) async-start(), calls=%async_computation.3 | async-start | bytes 2162688 | tf_op jit(solution)/shard_map/all_gather | solution.py:19
  230.3 166.8 %all-gather.9.cloned.1.call-start = ((), (), s32[]{:S(2)}) async-start(), calls=%async_computation.7 | async-start | bytes 2162688 | tf_op jit(solution)/shard_map/all_gather | solution.py:19
  281.4 200.1 %all-gather.11.cloned.1.call-start = ((), (), s32[]{:S(2)}) async-start(), calls=%async_computation.8 | async-start | bytes 2162688 | tf_op jit(solution)/shard_map/all_gather | solution.py:19
  317.1 797.2 %all-reduce.7.cloned.1.call-start = ((), (), s32[]{:S(2)}) async-start(), calls=%async_computation.5 | async-start | bytes 131072 | tf_op jit(solution)/shard_map/psum | solution.py:249
  571.8 8.4 copy-start.9
  940.2 395.6 %reduce-scatter.3.cloned.1.call-start = ((), (), s32[]{:S(2)}) async-start(), calls=%async_computation.4 | async-start | bytes 540672 | tf_op jit(solution)/shard_map/reduce_scatter | solution.py:218
  941.2 616.8 %reduce-scatter.5.cloned.1.call-start = ((), (), s32[]{:S(2)}) async-start(), calls=%async_computation.6 | async-start | bytes 540672 | tf_op jit(solution)/shard_map/reduce_scatter | solution.py:219
  943.6 145.7 %copy-start.23 = (f32[16,512]{1,0:T(8,128)S(1)}, f32[16,512]{1,0:T(8,128)}, u32[]{:S(2)}) copy-start(f32[16,512]{1,0:T(8,128)} %param.30) | copy-start | bytes 98308
  943.6 146.3 %copy-start.27 = (f32[1,512]{1,0:T(1,128)S(1)}, f32[1,512]{1,0:T(1,128)}, u32[]{:S(2)}) copy-start(f32[1,512]{1,0:T(1,128)} %copy-done.26) | copy-start | bytes 6148
  943.6 146.3 %copy-start.29 = (f32[1,512]{1,0:T(1,128)S(1)}, f32[1,512]{1,0:T(1,128)}, u32[]{:S(2)}) copy-start(f32[1,512]{1,0:T(1,128)} %copy-done.28) | copy-start | bytes 6148
  943.6 146.3 %copy-start.31 = (f32[1,512]{1,0:T(1,128)S(1)}, f32[1,512]{1,0:T(1,128)}, u32[]{:S(2)}) copy-start(f32[1,512]{1,0:T(1,128)} %copy-done.30) | copy-start | bytes 6148
  943.6 146.3 %copy-start.33 = (f32[1,512]{1,0:T(1,128)S(1)}, f32[1,512]{1,0:T(1,128)}, u32[]{:S(2)}) copy-start(f32[1,512]{1,0:T(1,128)} %copy-done.32) | copy-start | bytes 6148
  946.7 143.3 %collective-permute-start.1 = (f32[2,3,512]{2,1,0:T(4,128)S(1)}, f32[2,3,512]{2,1,0:T(4,128)S(1)}, u32[]{:S(2)}, u32[]{:S(2)}) collective-permute-start(f32[2,3,512]{2,1,0:T(4,128)S(1)} %slice.947), channel_id=1, source_target_pairs={{16,0},{32,16},{48,32},{64,48},{80,64},{96,80},{112,96},{128,112},... | collective-permute-start | bytes 36872 | tf_op jit(solution)/shard_map/ppermute | solution.py:12
  (248 other events, 1352.3 us)
Sparse Core Ops, SparseCore 0:
  95.8 132.3 all-reduce.4
  232.4 80.2 all-gather.6
  316.3 80.7 all-gather.8
  400.7 80.7 all-gather.10
  940.4 173.8 all-reduce.6
  1119.7 216.0 reduce-scatter.2
  1340.7 217.1 reduce-scatter.4
where the time goes:
time: 1580 us; the launch traced here: 1570 us
  waiting for transfers between devices  734 us (46%)
  blocking collectives  269 us (17%)
  local copies, waits for them, and re-layouts  257 us (16%)
  other arithmetic  232 us (15%)
  loops' own time  49.1 us (3%)
    reduce_scatter x1, waiting for transfers between devices, body(): lax.psum_scatter(contract_first(dt_low, grad_dt_round), 'dp', scatter_dim...  222 us
    reduce_scatter x1, waiting for transfers between devices, body(): lax.psum_scatter(proj_terms[:low_rank], 'dp', scatter_dimension=0, tiled=...  222 us
    psum x1, blocking collectives, body(): lax.psum((proj_terms[low_rank:], conv_terms, jnp.sum(grad_preact, axis=(0...  141 us
    all_gather x3, waiting for transfers between devices, prefix(): gathered = jax.tree.map(lambda a: lax.all_gather(a, axis), part)  136 us
    psum x1, waiting for transfers between devices, body(): projected = lax.psum(contract_last(x_flat, proj_full), 'expert')  131 us
    reduce_sum x64, other arithmetic, one_turn(): jnp.sum(prev_term * decay_rate[None], axis=1)  69.3 us
    psum x1, blocking collectives, body(): grad_projected = lax.psum(grad_partial, 'expert').astype(jnp.bfloat16)  49.8 us
    dynamic_slice x64, local copies, waits for them, and re-layouts, run_forward(): lax.scan(one_turn, begin_state, jnp.arange(turn_count, dtype=jnp.int32))  48 us
  transfers between devices with their start and end apart: 9, of which 6 were waited for; matrix products, arithmetic and copies ran while one was open for 7% of the time, Pallas kernels for 0%

commit v1 on v0

v1 whole, which is shorter than its diff:
```python
import functools

import jax
import jax.numpy as jnp
import numpy as np
from jax import lax
from jax.experimental import pallas as pl
from jax.experimental.pallas import tpu as pltpu
from jax.sharding import PartitionSpec as P

F32 = jnp.float32
BF16 = jnp.bfloat16
MESH = pl.DeviceIdType.MESH
LANES = 128
CHUNK = 16
VMEM_BYTES = 56 * 1024 * 1024

whole = pl.BlockSpec(memory_space=pltpu.VMEM)
sds = jax.ShapeDtypeStruct


def dot_nn(left, right, precision=None):
    return lax.dot_general(
        left, right, (((1,), (0,)), ((), ())), preferred_element_type=F32, precision=precision
    )


def dot_nt(left, right, precision=None):
    return lax.dot_general(
        left, right, (((1,), (1,)), ((), ())), preferred_element_type=F32, precision=precision
    )


def dot_tn(left, right):
    return lax.dot_general(left, right, (((0,), (0,)), ((), ())), preferred_element_type=F32)


def greet(axis, count):
    me = lax.axis_index(axis)
    barrier = pltpu.get_barrier_semaphore()

    def hail(k, carry):
        pl.semaphore_signal(
            barrier, inc=1, device_id={axis: lax.rem(me + k, count)}, device_id_type=MESH
        )
        return carry

    lax.fori_loop(1, count, hail, 0)
    pl.semaphore_wait(barrier, count - 1)
    return me


def send_all(axis, count, me, source, landing, send_sem, recv_sem):
    def one(k, carry):
        peer = lax.rem(me + k, count)
        pltpu.make_async_remote_copy(
            src_ref=source(peer),
            dst_ref=landing(me),
            send_sem=send_sem.at[k],
            recv_sem=recv_sem.at[k],
            device_id={axis: peer},
            device_id_type=MESH,
        ).start()
        return carry

    lax.fori_loop(1, count, one, 0)


def wait_all(axis, count, me, source, landing, send_sem, recv_sem, sent):
    def one(k, carry):
        peer = lax.rem(me + k, count)
        origin = lax.rem(me + count - k, count)
        copy = pltpu.make_async_remote_copy(
            src_ref=source(peer),
            dst_ref=landing(origin),
            send_sem=send_sem.at[k],
            recv_sem=recv_sem.at[k],
            device_id={axis: peer},
            device_id_type=MESH,
        )
        if sent:
            copy.wait_send()
        else:
            copy.wait_recv()
        return carry

    lax.fori_loop(1, count, one, 0)


class Exchange:
    def __init__(self, axis, count, me, source, landing, sems):
        self.args = (axis, count, me, source, landing, sems[0], sems[1])

    def start(self):
        send_all(*self.args)

    def wait_recv(self):
        wait_all(*self.args, False)

    def wait_send(self):
        wait_all(*self.args, True)


def pair_sems(count):
    return [pltpu.SemaphoreType.DMA((count,)), pltpu.SemaphoreType.DMA((count,))]


def comm_params(number):
    return pltpu.CompilerParams(
        collective_id=number, has_side_effects=True, vmem_limit_bytes=VMEM_BYTES
    )


def gather_body(count, block, extra, edge, block_all, extra_all, edge_in, s0, s1, s2, s3, s4, s5):
    me = greet("dp", count)
    halo = pltpu.make_async_remote_copy(
        src_ref=edge,
        dst_ref=edge_in,
        send_sem=s4,
        recv_sem=s5,
        device_id={"dp": lax.rem(me + 1, count)},
        device_id_type=MESH,
    )
    halo.start()
    first = Exchange("dp", count, me, lambda p: block, lambda d: block_all.at[d], (s0, s1))
    second = Exchange("dp", count, me, lambda p: extra, lambda d: extra_all.at[d], (s2, s3))
    first.start()
    second.start()
    block_all[me] = block[...]
    extra_all[me] = extra[...]
    halo.wait()
    first.wait_recv()
    second.wait_recv()
    first.wait_send()
    second.wait_send()


def gather_weights(block, extra, edge, count):
    return pl.pallas_call(
        functools.partial(gather_body, count),
        out_shape=(
            sds((count,) + block.shape, block.dtype),
            sds((count,) + extra.shape, extra.dtype),
            sds(edge.shape, edge.dtype),
        ),
        in_specs=[whole] * 3,
        out_specs=(whole,) * 3,
        scratch_shapes=pair_sems(count)
        + pair_sems(count)
        + [pltpu.SemaphoreType.DMA, pltpu.SemaphoreType.DMA],
        compiler_params=comm_params(1),
        name="gather_weights",
    )(block, extra, edge)


def reduce_body(count, low, bc, low_all, bc_all, low_slots, bc_slots, s0, s1, s2, s3, s4, s5, s6, s7):
    me = greet("expert", count)
    first = Exchange(
        "expert", count, me, lambda p: low.at[p], lambda d: low_slots.at[d], (s0, s1)
    )
    second = Exchange("expert", count, me, lambda p: bc.at[p], lambda d: bc_slots.at[d], (s2, s3))
    first.start()
    second.start()
    low_slots[me] = low[me]
    bc_slots[me] = bc[me]
    first.wait_recv()
    second.wait_recv()

    def add(k, total):
        return (total[0] + low_slots[k].astype(F32), total[1] + bc_slots[k])

    zero = (jnp.zeros(low.shape[1:], F32), jnp.zeros(bc.shape[1:], F32))
    low_sum, bc_sum = lax.fori_loop(0, count, add, zero)
    low_all[me] = low_sum.astype(BF16)
    bc_all[me] = bc_sum
    third = Exchange(
        "expert", count, me, lambda p: low_all.at[me], lambda d: low_all.at[d], (s4, s5)
    )
    fourth = Exchange(
        "expert", count, me, lambda p: bc_all.at[me], lambda d: bc_all.at[d], (s6, s7)
    )
    third.start()
    fourth.start()
    first.wait_send()
    second.wait_send()
    third.wait_recv()
    fourth.wait_recv()
    third.wait_send()
    fourth.wait_send()


def reduce_expert(low, bc, count, number):
    return pl.pallas_call(
        functools.partial(reduce_body, count),
        out_shape=(sds(low.shape, low.dtype), sds(bc.shape, bc.dtype)),
        in_specs=[whole] * 2,
        out_specs=(whole,) * 2,
        scratch_shapes=[pltpu.VMEM(low.shape, low.dtype), pltpu.VMEM(bc.shape, bc.dtype)]
        + pair_sems(count) * 4,
        compiler_params=comm_params(number),
        name="reduce_expert",
    )(low, bc)


def carry_body(count, parts, incoming, slots, found, s0, s1, s2, s3):
    me = greet("dp", count)
    first = Exchange("dp", count, me, lambda p: parts.at[p], lambda d: slots.at[d], (s0, s1))
    first.start()
    slots[me] = parts[me]
    first.wait_recv()

    def one(k, carried):
        ahead, behind = carried
        late = count - 1 - k
        found[k, 0:1, :] = ahead
        found[late, 1:2, :] = behind
        ahead = slots[k, 2:3, :] * ahead + slots[k, 0:1, :]
        behind = slots[late, 2:3, :] * behind + slots[late, 1:2, :]
        return (ahead, behind)

    zero = jnp.zeros((1, parts.shape[2]), F32)
    lax.fori_loop(0, count, one, (zero, zero))
    second = Exchange("dp", count, me, lambda p: found.at[p], lambda d: incoming.at[d], (s2, s3))
    second.start()
    incoming[me] = found[me]
    first.wait_send()
    second.wait_recv()
    second.wait_send()


def exchange_carries(parts, count):
    rows, width = parts.shape[0], parts.shape[2]
    return pl.pallas_call(
        functools.partial(carry_body, count),
        out_shape=sds((rows, 2, width), F32),
        in_specs=[whole],
        out_specs=whole,
        scratch_shapes=[pltpu.VMEM(parts.shape, F32), pltpu.VMEM((rows, 2, width), F32)]
        + pair_sems(count) * 2,
        compiler_params=comm_params(3),
        name="exchange_carries",
    )(parts)


def finish_body(
    count, big, small, edge, low_out, dt_out, small_all, edge_in, big_slots, small_slots,
    s0, s1, s2, s3, s4, s5, s6, s7,
):
    me = greet("dp", count)
    halo = pltpu.make_async_remote_copy(
        src_ref=edge,
        dst_ref=edge_in,
        send_sem=s6,
        recv_sem=s7,
        device_id={"dp": lax.rem(me + count - 1, count)},
        device_id_type=MESH,
    )
    halo.start()
    second = Exchange(
        "dp", count, me, lambda p: small.at[p], lambda d: small_slots.at[d], (s2, s3)
    )
    first = Exchange("dp", count, me, lambda p: big.at[p], lambda d: big_slots.at[d], (s0, s1))
    second.start()
    first.start()
    small_slots[me] = small[me]
    big_slots[me] = big[me]
    second.wait_recv()

    def add_small(k, total):
        return total + small_slots[k]

    small_all[me] = lax.fori_loop(0, count, add_small, jnp.zeros(small.shape[1:], F32))
    third = Exchange(
        "dp", count, me, lambda p: small_all.at[me], lambda d: small_all.at[d], (s4, s5)
    )
    third.start()
    first.wait_recv()

    def add_big(k, total):
        return total + big_slots[k].astype(F32)

    total = lax.fori_loop(0, count, add_big, jnp.zeros(big.shape[1:], F32))
    half = big.shape[1] // 2
    low_out[...] = total[:half]
    dt_out[...] = total[half:]
    halo.wait()
    third.wait_recv()
    second.wait_send()
    first.wait_send()
    third.wait_send()


def finish_sums(big, small, edge, count):
    half, width = big.shape[1] // 2, big.shape[2]
    return pl.pallas_call(
        functools.partial(finish_body, count),
        out_shape=(
            sds((half, width), F32),
            sds((half, width), F32),
            sds(small.shape, F32),
            sds(edge.shape, F32),
        ),
        in_specs=[whole] * 3,
        out_specs=(whole,) * 4,
        scratch_shapes=[pltpu.VMEM(big.shape, big.dtype), pltpu.VMEM(small.shape, F32)]
        + pair_sems(count) * 3
        + [pltpu.SemaphoreType.DMA, pltpu.SemaphoreType.DMA],
        compiler_params=comm_params(5),
        name="finish_sums",
    )(big, small, edge)


def local_call(body, outs, scratch, name, *args):
    return pl.pallas_call(
        body,
        out_shape=outs,
        in_specs=[whole] * len(args),
        out_specs=(whole,) * len(outs),
        scratch_shapes=scratch,
        compiler_params=pltpu.CompilerParams(vmem_limit_bytes=VMEM_BYTES),
        name=name,
    )(*args)


def conv_body(
    xin, front, block_all, extra_all, pick_dt, pick_low, pick_extra, weight, bias,
    preact_out, xconv_out, low_out, bc_out, proj_out, dt_out, padded, extra,
):
    seqs, tokens, width = xin.shape
    taps = weight.shape[0]
    devices = extra_all.shape[0]
    for i in range(devices):
        extra[i : i + 1, :] = extra_all[i]
    gathered = block_all[...].reshape(devices * block_all.shape[1], width)
    dt_out[...] = dot_nn(pick_dt[...], gathered).astype(BF16)
    proj = (
        dot_nn(pick_low[...], gathered) + dot_nn(pick_extra[...], extra[...].astype(BF16))
    ).astype(BF16)
    proj_out[...] = proj
    keep = jnp.where(lax.axis_index("dp") == 0, 0.0, 1.0).astype(F32)
    lead = front[...].astype(F32) * keep
    for s in range(seqs):
        padded[s, 8 - (taps - 1) : 8, :] = lead[s * (taps - 1) : (s + 1) * (taps - 1), :]
        padded[s, 8:, :] = xin[s].astype(F32)
        preact = bias[...] + jnp.zeros((tokens, width), F32)
        for k in range(taps):
            begin = 8 - (taps - 1) + k
            preact = preact + weight[k : k + 1, :] * padded[s, begin : begin + tokens, :]
        rows = slice(s * tokens, (s + 1) * tokens)
        preact_out[rows, :] = preact
        xconv_out[rows, :] = (preact * lax.logistic(preact)).astype(BF16)
    x_flat = xconv_out[...]
    rank = dt_out.shape[0]
    low_out[...] = dot_nt(x_flat, proj[:rank]).reshape(low_out.shape).astype(BF16)
    bc = dot_nt(proj[rank:], x_flat)
    per = bc_out.shape[1]
    for e in range(bc_out.shape[0]):
        bc_out[e] = bc[e * per : (e + 1) * per, :]


def decay_of(step_row, rate):
    return jnp.exp(step_row * rate)


def views(refs, first, count, lanes):
    first = pl.multiple_of(first, count)
    return [ref.at[pl.ds(first, count), lanes] for ref in refs]


def local_body(
    low_all, bc_all, dt_weight, dt_bias, a_log, xconv, zin, cot,
    pre_out, step_out, gy_out, bx_out, cx_out, parts_out, bc_rows, u_rows,
):
    seqs, tokens, width = zin.shape
    states = a_log.shape[0]
    rows = seqs * tokens
    low = low_all[...].reshape(rows, low_all.shape[2])
    pre = dot_nn(low, dt_weight[...]) + dt_bias[...]
    pre_out[...] = pre
    step = jnp.maximum(pre, 0.0) + jnp.log1p(jnp.exp(-jnp.abs(pre)))
    step_out[...] = step
    u_rows[...] = step * xconv[...].astype(F32)
    per = bc_all.shape[1]
    for e in range(bc_all.shape[0]):
        bc_rows[e * per : (e + 1) * per, :] = bc_all[e]
    for s in range(seqs):
        z = zin[s].astype(F32)
        gy_out[s * tokens : (s + 1) * tokens, :] = cot[s].astype(F32) * z * lax.logistic(z)
    for r in range(rows):
        bx_out[r] = jnp.broadcast_to(bc_rows[0:states, r : r + 1], (states, LANES))
        cx_out[r] = jnp.broadcast_to(bc_rows[states : 2 * states, r : r + 1], (states, LANES))
    rate_all = -jnp.exp(a_log[...])
    chunk = 8
    for block in range(width // LANES):
        lanes = slice(block * LANES, (block + 1) * LANES)
        rate = rate_all[:, lanes]

        def one(k, carried):
            ahead = list(carried[:seqs])
            behind = list(carried[seqs:])
            for s in range(seqs):
                first = s * tokens + k * chunk
                last = s * tokens + tokens - (k + 1) * chunk
                step_f, u_f = views((step_out, u_rows), first, chunk, lanes)
                step_b, gy_b = views((step_out, gy_out), last, chunk, lanes)
                for i in range(chunk):
                    now = decay_of(step_f[i : i + 1, :], rate)
                    ahead[s] = now * ahead[s] + bx_out[first + i] * u_f[i : i + 1, :]
                    j = chunk - 1 - i
                    now = decay_of(step_b[j : j + 1, :], rate)
                    behind[s] = now * (cx_out[last + j] * gy_b[j : j + 1, :] + behind[s])
            return tuple(ahead + behind)

        zero = jnp.zeros((states, LANES), F32)
        ends = lax.fori_loop(0, tokens // chunk, one, (zero,) * (2 * seqs))
        for s in range(seqs):
            total = jnp.sum(step[s * tokens : (s + 1) * tokens, lanes], axis=0, keepdims=True)
            passing = jnp.exp(rate * total)
            for n in range(states):
                parts_out[s * states + n, 0:1, lanes] = ends[s][n : n + 1, :]
                parts_out[s * states + n, 1:2, lanes] = ends[seqs + s][n : n + 1, :]
                parts_out[s * states + n, 2:3, lanes] = passing[n : n + 1, :]


def main_body(
    step, pre, xconv, gy, zin, cot, bx, cx, bc_all, a_log, d_skip, incoming, dt_weight, low_all,
    gate_out, low_out, bc_out, dtw_out, base_out, sums_out,
    bc_rows, begin, hist, adjoint, prevs, u_rows, y_rows, b_rows, q_rows, fold_b, fold_c,
):
    seqs, tokens, width = zin.shape
    states = a_log.shape[0]
    rows = seqs * tokens
    span = CHUNK * states
    turns = tokens // CHUNK
    per = bc_all.shape[1]
    for e in range(bc_all.shape[0]):
        bc_rows[e * per : (e + 1) * per, :] = bc_all[e]
    for s in range(seqs):
        for n in range(states):
            begin[s, n : n + 1, :] = incoming[s * states + n, 0:1, :]
            begin[seqs + s, n : n + 1, :] = incoming[s * states + n, 1:2, :]
        hist[s, 0] = begin[s].astype(BF16)
    u_rows[...] = step[...] * xconv[...].astype(F32)
    rate_all = -jnp.exp(a_log[...])
    spread = (
        (lax.broadcasted_iota(jnp.int32, (states, span), 1) & (states - 1))
        == lax.broadcasted_iota(jnp.int32, (states, span), 0)
    ).astype(F32)
    spread_half = spread.astype(BF16)
    own = (
        lax.broadcasted_iota(jnp.int32, (rows, span), 1) // states
        == (lax.broadcasted_iota(jnp.int32, (rows, span), 0) & (CHUNK - 1))
    ).astype(F32)
    across = jnp.transpose(bc_rows[...])
    b_diag = (dot_nn(across[:, :states].astype(BF16), spread_half) * own).astype(BF16)
    c_diag = (dot_nn(across[:, states:].astype(BF16), spread_half) * own).astype(BF16)
    fold = own[:CHUNK].astype(BF16)
    gy_half = gy[...].astype(BF16)
    u_half = u_rows[...].astype(BF16)

    for block in range(width // LANES):
        lanes = slice(block * LANES, (block + 1) * LANES)
        rate = rate_all[:, lanes]

        def forward(k, carried):
            carried = list(carried)
            t = k * CHUNK
            for s in range(seqs):
                step_v, u_v = views((step, u_rows), s * tokens + t, CHUNK, lanes)
                for i in range(CHUNK):
                    now = decay_of(step_v[i : i + 1, :], rate)
                    carried[s] = now * carried[s] + bx[s * tokens + t + i] * u_v[i : i + 1, :]
                    hist[s, t + i + 1, :, lanes] = carried[s].astype(BF16)
            return tuple(carried)

        lax.fori_loop(0, turns, forward, tuple(begin[s, :, lanes] for s in range(seqs)))

        def backward(k, carried):
            passed = list(carried[:seqs])
            rate_grad = carried[seqs]
            first = tokens - (k + 1) * CHUNK
            for s in range(seqs):
                step_v, gy_v = views((step, gy), s * tokens + first, CHUNK, lanes)
                for i in reversed(range(CHUNK)):
                    t = first + i
                    step_row = step_v[i : i + 1, :]
                    now = decay_of(step_row, rate)
                    adj = cx[s * tokens + t] * gy_v[i : i + 1, :] + passed[s]
                    adjoint[s, t, :, lanes] = adj.astype(BF16)
                    passed[s] = now * adj
                    prev = passed[s] * hist[s, t, :, lanes].astype(F32) * rate
                    prevs[s, t, :, lanes] = prev.astype(BF16)
                    rate_grad = rate_grad + prev * step_row
            return tuple(passed) + (rate_grad,)

        ends = lax.fori_loop(
            0,
            turns,
            backward,
            tuple(begin[seqs + s, :, lanes] for s in range(seqs))
            + (jnp.zeros((states, LANES), F32),),
        )
        sums_out[0:states, lanes] = ends[seqs]

    for s in range(seqs):
        for k in range(turns):
            t = k * CHUNK
            here = slice(s * tokens + t, s * tokens + t + CHUNK)
            history = hist[s, t + 1 : t + 1 + CHUNK].reshape(span, width)
            y_rows[here, :] = dot_nn(c_diag[here], history)
            fold_c[here, :] = dot_nt(gy_half[here], history) * own[:CHUNK]
            adj = adjoint[s, t : t + CHUNK].reshape(span, width)
            b_rows[here, :] = dot_nn(b_diag[here], adj)
            fold_b[here, :] = dot_nt(u_half[here], adj) * own[:CHUNK]
            q_rows[here, :] = dot_nn(fold, prevs[s, t : t + CHUNK].reshape(span, width))

    exact = lax.Precision.HIGHEST
    grad_b = dot_nt(spread, fold_b[...], exact)
    grad_c = dot_nt(spread, fold_c[...], exact)
    grad_bc = jnp.concatenate([grad_b, grad_c], 0)
    for e in range(bc_out.shape[0]):
        bc_out[e] = grad_bc[e * per : (e + 1) * per, :]

    x = xconv[...].astype(F32)
    for s in range(seqs):
        here = slice(s * tokens, (s + 1) * tokens)
        z = zin[s].astype(F32)
        sig = lax.logistic(z)
        y_value = y_rows[here, :] + d_skip[...] * x[here]
        gate_out[s] = (cot[s].astype(F32) * y_value * sig * (1.0 + z * (1.0 - sig))).astype(BF16)
    b_adjoint = b_rows[...]
    grad_pre = (x * b_adjoint + q_rows[...]) * lax.logistic(pre[...])
    grad_round = grad_pre.astype(BF16)
    base_out[...] = d_skip[...] * gy[...] + step[...] * b_adjoint
    low_out[...] = dot_nt(grad_round, dt_weight[...]).reshape(low_out.shape).astype(BF16)
    low = low_all[...].reshape(rows, low_all.shape[2])
    dtw_out[...] = dot_tn(low, grad_round)
    sums_out[states : states + 1, :] = jnp.sum(grad_pre, axis=0, keepdims=True)
    sums_out[states + 1 : states + 2, :] = jnp.sum(gy[...] * x, axis=0, keepdims=True)


def last_body(
    low_all, bc_all, xconv, proj, base, preact, xin, front, weight, dtw, sums,
    big_out, small_out, edge_out, gradx_out, tail_out, padded, grads, bc_rows,
):
    seqs, tokens, width = xin.shape
    taps = weight.shape[0]
    reach = taps - 1
    rows = seqs * tokens
    rank = low_all.shape[2]
    per = bc_all.shape[1]
    for e in range(bc_all.shape[0]):
        bc_rows[e * per : (e + 1) * per, :] = bc_all[e]
    low = low_all[...].reshape(rows, rank)
    bc = bc_rows[...].astype(BF16)
    x_flat = xconv[...]
    low_terms = dot_tn(low, x_flat)
    for i in range(big_out.shape[0]):
        part = big_out.shape[1] // 2
        big_out[i] = jnp.concatenate(
            [low_terms[i * part : (i + 1) * part], dtw[i * part : (i + 1) * part, :]], 0
        ).astype(BF16)
    state_terms = dot_nn(bc, x_flat)
    across = jnp.transpose(bc_rows[...]).astype(BF16)
    grad_conv = base[...] + dot_nn(low, proj[0:rank, :]) + dot_nn(across, proj[rank:, :])
    pre = preact[...]
    sig = lax.logistic(pre)
    grad_pre = grad_conv * sig * (1.0 + pre * (1.0 - sig))
    keep = jnp.where(lax.axis_index("dp") == 0, 0.0, 1.0).astype(F32)
    lead = front[...].astype(F32) * keep
    conv_terms = [jnp.zeros((1, width), F32) for k in range(taps)]
    edge_out[...] = jnp.zeros(edge_out.shape, F32)
    tail_out[...] = jnp.zeros(tail_out.shape, F32)
    for s in range(seqs):
        mine = grad_pre[s * tokens : (s + 1) * tokens]
        padded[s, 8 - reach : 8, :] = lead[s * reach : (s + 1) * reach, :]
        padded[s, 8:, :] = xin[s].astype(F32)
        grads[s, 0:tokens, :] = mine
        grads[s, tokens:, :] = jnp.zeros((8, width), F32)
        edge_out[s * reach : (s + 1) * reach, :] = mine[0:reach]
        result = jnp.zeros((tokens, width), F32)
        for k in range(taps):
            begin = 8 - reach + k
            conv_terms[k] = conv_terms[k] + jnp.sum(
                mine * padded[s, begin : begin + tokens, :], axis=0, keepdims=True
            )
            late = reach - k
            result = result + weight[k : k + 1, :] * grads[s, late : late + tokens, :]
        gradx_out[s] = result.astype(BF16)
        tail_out[s * reach : (s + 1) * reach, :] = result[tokens - reach :]
    states2 = bc.shape[0]
    extra = sums.shape[0]
    pieces = [state_terms[i : i + 1] for i in range(states2)]
    pieces += conv_terms
    pieces.append(jnp.sum(grad_pre, axis=0, keepdims=True))
    pieces += [sums[i : i + 1, :] for i in range(extra)]
    while len(pieces) < 2 * small_out.shape[0]:
        pieces.append(jnp.zeros((1, width), F32))
    for i, piece in enumerate(pieces):
        small_out[i // 2, i % 2 : i % 2 + 1, :] = piece


def body(
    xin, zin, cotangent, conv_weight, conv_bias, proj_weight, dt_weight, dt_bias, a_log, d_skip
):
    dp = lax.axis_size("dp")
    expert = lax.axis_size("expert")
    seqs, tokens, width = xin.shape
    taps = conv_weight.shape[0]
    reach = taps - 1
    states = a_log.shape[0]
    rows = seqs * tokens
    low_rows = dt_weight.shape[0]
    proj_rows = proj_weight.shape[0]
    rank = low_rows * dp
    total_rows = proj_rows * dp

    block = jnp.concatenate([dt_weight, proj_weight[:low_rows]], 0)
    extra = proj_weight[low_rows:].astype(F32)
    edge = jnp.pad(
        xin[:, tokens - reach :, :].reshape(seqs * reach, width), ((0, 16 - seqs * reach), (0, 0))
    )
    block_all, extra_all, front = gather_weights(block, extra, edge, dp)

    pick_dt = np.zeros((rank, 2 * rank), np.float32)
    pick_low = np.zeros((total_rows, 2 * rank), np.float32)
    pick_extra = np.zeros((total_rows, dp), np.float32)
    for i in range(dp):
        for j in range(low_rows):
            pick_dt[i * low_rows + j, i * 2 * low_rows + j] = 1.0
            pick_low[i * proj_rows + j, i * 2 * low_rows + low_rows + j] = 1.0
        pick_extra[i * proj_rows + low_rows, i] = 1.0

    low_shape = (expert, rows // expert, rank)
    bc_shape = (expert, 2 * states // expert, rows)
    flat = (rows, width)
    preact, xconv, low_part, bc_part, proj_full, dt_full = local_call(
        conv_body,
        (
            sds(flat, F32),
            sds(flat, BF16),
            sds(low_shape, BF16),
            sds(bc_shape, F32),
            sds((total_rows, width), BF16),
            sds((rank, width), BF16),
        ),
        [pltpu.VMEM((seqs, tokens + 8, width), F32), pltpu.VMEM((dp, width), F32)],
        "conv_project",
        xin,
        front,
        block_all,
        extra_all,
        jnp.asarray(pick_dt, BF16),
        jnp.asarray(pick_low, BF16),
        jnp.asarray(pick_extra, BF16),
        conv_weight,
        conv_bias[None, :],
    )
    low_all, bc_all = reduce_expert(low_part, bc_part, expert, 2)

    wide = (rows, states, LANES)
    pre, step, gy, bx, cx, parts = local_call(
        local_body,
        (
            sds(flat, F32),
            sds(flat, F32),
            sds(flat, F32),
            sds(wide, F32),
            sds(wide, F32),
            sds((seqs * states, 3, width), F32),
        ),
        [pltpu.VMEM((2 * states, rows), F32), pltpu.VMEM(flat, F32)],
        "local_scans",
        low_all,
        bc_all,
        dt_full,
        dt_bias[None, :],
        a_log,
        xconv,
        zin,
        cotangent,
    )
    incoming = exchange_carries(parts, dp)

    gate, low_grad, bc_grad, dtw, base, sums = local_call(
        main_body,
        (
            sds((seqs, tokens, width), BF16),
            sds(low_shape, BF16),
            sds(bc_shape, F32),
            sds((rank, width), F32),
            sds(flat, F32),
            sds((states + 2, width), F32),
        ),
        [
            pltpu.VMEM((2 * states, rows), F32),
            pltpu.VMEM((2 * seqs, states, width), F32),
            pltpu.VMEM((seqs, tokens + 1, states, width), BF16),
            pltpu.VMEM((seqs, tokens, states, width), BF16),
            pltpu.VMEM((seqs, tokens, states, width), BF16),
            pltpu.VMEM(flat, F32),
            pltpu.VMEM(flat, F32),
            pltpu.VMEM(flat, F32),
            pltpu.VMEM(flat, F32),
            pltpu.VMEM((rows, CHUNK * states), F32),
            pltpu.VMEM((rows, CHUNK * states), F32),
        ],
        "full_scans",
        step,
        pre,
        xconv,
        gy,
        zin,
        cotangent,
        bx,
        cx,
        bc_all,
        a_log,
        d_skip[None, :],
        incoming,
        dt_full,
        low_all,
    )
    low_sum, bc_sum = reduce_expert(low_grad, bc_grad, expert, 4)

    big, small, edge_grad, grad_x, tail = local_call(
        last_body,
        (
            sds((dp, 2 * low_rows, width), BF16),
            sds((dp, 2, width), F32),
            sds((8, width), F32),
            sds((seqs, tokens, width), BF16),
            sds((8, width), F32),
        ),
        [
            pltpu.VMEM((seqs, tokens + 8, width), F32),
            pltpu.VMEM((seqs, tokens + 8, width), F32),
            pltpu.VMEM((2 * states, rows), F32),
        ],
        "weight_grads",
        low_sum,
        bc_sum,
        xconv,
        proj_full,
        base,
        preact,
        xin,
        front,
        conv_weight,
        dtw,
        sums,
    )
    grad_low, grad_dtw, small_all, after = finish_sums(big, small, edge_grad, dp)

    after = jnp.where(lax.axis_index("dp") == dp - 1, 0.0, after)
    after = after[: seqs * reach].reshape(seqs, reach, width)
    ends = tail[: seqs * reach].reshape(seqs, reach, width)
    fixed = []
    for i in range(reach):
        row = ends[:, i]
        for k in range(taps):
            source = i + (reach - k) - reach
            if source >= 0:
                row = row + conv_weight[k][None, :] * after[:, source]
        fixed.append(row)
    grad_x = lax.dynamic_update_slice(
        grad_x, jnp.stack(fixed, 1).astype(BF16), (0, tokens - reach, 0)
    )
    table = small_all.reshape(2 * dp, width)
    at = 2 * states
    return (
        grad_x,
        gate,
        grad_low,
        table[:at],
        grad_dtw,
        table[at : at + taps],
        table[at + taps],
        table[at + taps + 1 + states],
        table[at + taps + 1 : at + taps + 1 + states],
        table[at + taps + 2 + states],
    )


def solution(mesh):
    return jax.shard_map(
        body,
        mesh=mesh,
        in_specs=(
            P(None, "dp", "expert"),
            P(None, "dp", "expert"),
            P(None, "dp", "expert"),
            P(None, "expert"),
            P("expert"),
            P("dp", "expert"),
            P("dp", "expert"),
            P("expert"),
            P(None, "expert"),
            P("expert"),
        ),
        out_specs=(
            P(None, "dp", "expert"),
            P(None, "dp", "expert"),
            P("dp", "expert"),
            P(None, "expert"),
            P("dp", "expert"),
            P(None, "expert"),
            P("expert"),
            P("expert"),
            P(None, "expert"),
            P("expert"),
        ),
        check_vma=False,
    )
```

time: 1580 us -> 181 us (0.11)
  waiting for transfers between devices: 734 us -> 0 us
  blocking collectives: 269 us -> 0 us
  local copies, waits for them, and re-layouts: 257 us -> 11.8 us
  other arithmetic: 232 us -> 3.36 us
  Pallas kernels: 0 us -> 164 us
  loops' own time: 49.1 us -> 0 us
    reduce_scatter x2 -> x0, waiting for transfers between devices: 444 us -> none  [the longest x1 222 us: body(): lax.psum_scatter(contract_first(dt_low, grad_dt_round), 'dp', scatter_dim...]
    psum x2 -> x0, blocking collectives: 191 us -> none  [the longest x1 141 us: body(): lax.psum((proj_terms[low_rank:], conv_terms, jnp.sum(grad_preact, axis=(0...]
    pallas_call x0 -> x9, Pallas kernels: none -> 164 us  [the longest x2 46.7 us: reduce_expert(): pl.pallas_call(functools.partial(reduce_body, count), out_shape=(sds(low....]
    psum x2 -> x0, waiting for transfers between devices: 154 us -> none  [the longest x1 131 us: body(): projected = lax.psum(contract_last(x_flat, proj_full), 'expert')]
    reduce_sum x164 -> x0, other arithmetic: 139 us -> none  [the longest x64 69.3 us: one_turn(): jnp.sum(prev_term * decay_rate[None], axis=1)]
    all_gather x3 -> x0, waiting for transfers between devices: 136 us -> none  [prefix(): gathered = jax.tree.map(lambda a: lax.all_gather(a, axis), part)]
    mul x112 -> x0, local copies, waits for them, and re-layouts: 105 us -> none  [the longest x32 43.5 us: one_turn(): adjoint = c_part[:, offset, :, None] * gy_part[:, offset, None, :] + passed]
    all_gather x2 -> x0, blocking collectives: 77.6 us -> none  [the longest x1 43 us: body(): lax.all_gather(proj_weight, 'dp', axis=0, tiled=True)]
  transfers between devices with their start and end apart: 9 -> 0, of which waited for: 6 -> 0; matrix products, arithmetic and copies ran while one was open for 7% -> 0% of each run, Pallas kernels for 0% -> 0%
where the time goes in v1:
time: 181 us; the launch traced here: 179 us
  Pallas kernels  164 us (91%)
  local copies, waits for them, and re-layouts  11.8 us (7%)
  other arithmetic  3.36 us (2%)
    pallas_call x2, Pallas kernels, reduce_expert(): pl.pallas_call(functools.partial(reduce_body, count), out_shape=(sds(low....  46.7 us
    pallas_call x4, Pallas kernels, local_call(): pl.pallas_call(body, out_shape=outs, in_specs=[whole] * len(args), out_sp...  32.4 us
    pallas_call x1, Pallas kernels, gather_weights(): pl.pallas_call(functools.partial(gather_body, count), out_shape=(sds((cou...  31.5 us
    pallas_call x1, Pallas kernels, finish_sums(): pl.pallas_call(functools.partial(finish_body, count), out_shape=(sds((hal...  29.1 us
    pallas_call x1, Pallas kernels, exchange_carries(): pl.pallas_call(functools.partial(carry_body, count), out_shape=sds((rows,...  23.9 us

profile of v1, /device:TPU:1, one launch (start us, length us, event | category | flops | bytes accessed | tf_op | source)
XLA Modules:
  0.0 179.4 jit_solution(3180195658296951868)
XLA Ops:
  0.6 0.7 slice.80
  2.0 0.7 slice.78
  2.7 1.3 pad_maximum_fusion.block
  4.0 1.3 slice_convert_fusion.extra
  5.3 31.5 %gather_weights.1 = (bf16[32,16,512]{2,1,0:T(8,128)(2,1)}, f32[32,1,512]{2,1,0:T(1,128)}, bf16[16,512]{1,0:T(8,128)(2,1)}) custom-call(bf16[16,512]{1,0:T(8,128)(2,1)} %pad_maximum_fusion.block, f32[1,512]{1,0:T(1,128)} %slice_convert_fusion.extra, bf16[16,512]{1,0:T(8,128)(2,1)} %pad.4.edge), custom_call_target="tpu_custom_call" | custom-call | tf_op jit(solution)/shard_map/gather_weights/pallas_call | solution.py:139
  36.8 3.2 %conv_project.1 = (f32[256,512]{1,0:T(8,128)}, bf16[256,512]{1,0:T(8,128)(2,1)}, bf16[16,16,256]{2,1,0:T(8,128)(2,1)}, f32[16,2,256]{2,1,0:T(2,128)}, bf16[288,5...) custom-call(bf16[2,128,512]{2,1,0:T(8,128)(2,1)} %xin.3, bf16[16,512]{1,0:T(8,128)(2,1)} %get-tuple-element.44.front, ...), custom_call_target="tpu_custom_call" | custom-call | tf_op jit(solution)/shard_map/conv_project/pallas_call | solution.py:314
  40.1 24.8 %reduce_expert.2 = (bf16[16,16,256]{2,1,0:T(8,128)(2,1)}, f32[16,2,256]{2,1,0:T(2,128)}) custom-call(bf16[16,16,256]{2,1,0:T(8,128)(2,1)} %get-tuple-element.47.low, f32[16,2,256]{2,1,0:T(2,128)} %get-tuple-element.48.bc), custom_call_target="tpu_custom_call" | custom-call | tf_op jit(solution)/shard_map/reduce_expert/pallas_call | solution.py:193
  64.9 9.8 %local_scans.1 = (f32[256,512]{1,0:T(8,128)}, f32[256,512]{1,0:T(8,128)}, f32[256,512]{1,0:T(8,128)}, f32[256,16,128]{2,1,0:T(8,128)}, f32[256,16,128]{2,1,0:T(8,128)}, /*index=5*/f32[32,3,512]{2,1,0:T(4,128)}) custom-call(bf16[16,16,256]{2,1,0:T(8,128)(2,1)} %get-tuple-element.49.low_all, f32[16,2,256]{2,1,0:T(2,128)} %get-tuple-element.50.bc_all, ...), custom_call_target="tpu_custom_call" | custom-call | tf_op jit(solution)/shard_map/local_scans/pallas_call | solution.py:314
  74.6 23.9 %exchange_carries.1.incoming = f32[32,2,512]{2,1,0:T(2,128)} custom-call(f32[32,3,512]{2,1,0:T(4,128)} %get-tuple-element.58.parts), custom_call_target="tpu_custom_call" | custom-call | tf_op jit(solution)/shard_map/exchange_carries/pallas_call | solution.py:233
  98.5 15.6 %full_scans.1 = (bf16[2,128,512]{2,1,0:T(8,128)(2,1)}, bf16[16,16,256]{2,1,0:T(8,128)(2,1)}, f32[16,2,256]{2,1,0:T(2,128)}, f32[256,512]{1,0:T(8,128)}, f32[256,512]{1,0:T(8,128)}, /*index=5*/f32[18,512]{1,0:T(8,128)}) custom-call(f32[256,512]{1,0:T(8,128)} %get-tuple-element.53.step, f32[256,512]{1,0:T(8,128)} %get-tuple-element.54.pre, ...), custom_call_target="tpu_custom_call" | custom-call | tf_op jit(solution)/shard_map/full_scans/pallas_call | solution.py:314
  114.1 21.8 %reduce_expert.3 = (bf16[16,16,256]{2,1,0:T(8,128)(2,1)}, f32[16,2,256]{2,1,0:T(2,128)}) custom-call(bf16[16,16,256]{2,1,0:T(8,128)(2,1)} %get-tuple-element.59.low, f32[16,2,256]{2,1,0:T(2,128)} %get-tuple-element.60.bc), custom_call_target="tpu_custom_call" | custom-call | tf_op jit(solution)/shard_map/reduce_expert/pallas_call | solution.py:193
  135.9 3.8 %weight_grads.1 = (bf16[32,16,512]{2,1,0:T(8,128)(2,1)}, f32[32,2,512]{2,1,0:T(2,128)}, f32[8,512]{1,0:T(8,128)}, bf16[2,128,512]{2,1,0:T(8,128)(2,1)}, f32[8,512]{1,0:T(8,128)}) custom-call(bf16[16,16,256]{2,1,0:T(8,128)(2,1)} %get-tuple-element.61.low_all, f32[16,2,256]{2,1,0:T(2,128)} %get-tuple-element.62.bc_all, ...), custom_call_target="tpu_custom_call" | custom-call | tf_op jit(solution)/shard_map/weight_grads/pallas_call | solution.py:314
  139.8 29.1 %finish_sums.1 = (f32[8,512]{1,0:T(8,128)}, f32[8,512]{1,0:T(8,128)}, f32[32,2,512]{2,1,0:T(2,128)}, f32[8,512]{1,0:T(8,128)}) custom-call(bf16[32,16,512]{2,1,0:T(8,128)(2,1)} %get-tuple-element.70.big, f32[32,2,512]{2,1,0:T(2,128)} %get-tuple-element.71.small, f32[8,512]{1,0:T(8,128)} %get-tuple-element.72.edge), custom_call_target="tpu_custom_call" | custom-call | tf_op jit(solution)/shard_map/finish_sums/pallas_call | solution.py:295
  168.9 0.7 slice_select_fusion
  169.6 0.7 reshape.71
  170.4 1.4 dynamic_update_slice.3
  171.8 1.0 reshape.73
  172.8 0.6 slice.112
  174.0 0.8 slice.95
  174.8 0.7 slice.96
  175.5 0.7 slice.97
  176.2 0.6 slice.98
  176.8 1.3 copy.26
  178.1 1.3 copy.27
  (9 shorter events, 1.3 us)
Async XLA Ops:
  114.1 56.2 %copy-start = (f32[4,512]{1,0:T(4,128)S(1)}, f32[4,512]{1,0:T(4,128)}, u32[]{:S(2)}) copy-start(f32[4,512]{1,0:T(4,128)} %weight.3) | copy-start | bytes 24580

commit v2 on v0

v2 whole, which is shorter than its diff:
```python
import functools

import jax
import jax.numpy as jnp
from jax import lax
from jax.experimental import pallas as pl
from jax.experimental.pallas import tpu as pltpu
from jax.sharding import PartitionSpec as P

F32 = jnp.float32
BF16 = jnp.bfloat16
MESH = pl.DeviceIdType.MESH
LANES = 128
CHUNK = 16
VMEM_BYTES = 56 * 1024 * 1024

whole = pl.BlockSpec(memory_space=pltpu.VMEM)
sds = jax.ShapeDtypeStruct


def dot_nn(left, right, precision=None):
    return lax.dot_general(
        left, right, (((1,), (0,)), ((), ())), preferred_element_type=F32, precision=precision
    )


def dot_nt(left, right, precision=None):
    return lax.dot_general(
        left, right, (((1,), (1,)), ((), ())), preferred_element_type=F32, precision=precision
    )


def dot_tn(left, right):
    return lax.dot_general(left, right, (((0,), (0,)), ((), ())), preferred_element_type=F32)


def hail(axis, count, me):
    barrier = pltpu.get_barrier_semaphore()

    def one(k, carry):
        pl.semaphore_signal(
            barrier, inc=1, device_id={axis: lax.rem(me + k, count)}, device_id_type=MESH
        )
        return carry

    lax.fori_loop(1, count, one, 0)


def send_all(axis, count, me, source, landing, send_sem, recv_sem):
    def one(k, carry):
        peer = lax.rem(me + k, count)
        pltpu.make_async_remote_copy(
            src_ref=source(peer),
            dst_ref=landing(me),
            send_sem=send_sem.at[k],
            recv_sem=recv_sem.at[k],
            device_id={axis: peer},
            device_id_type=MESH,
        ).start()
        return carry

    lax.fori_loop(1, count, one, 0)


def wait_all(axis, count, me, source, landing, send_sem, recv_sem, sent):
    def one(k, carry):
        peer = lax.rem(me + k, count)
        origin = lax.rem(me + count - k, count)
        copy = pltpu.make_async_remote_copy(
            src_ref=source(peer),
            dst_ref=landing(origin),
            send_sem=send_sem.at[k],
            recv_sem=recv_sem.at[k],
            device_id={axis: peer},
            device_id_type=MESH,
        )
        if sent:
            copy.wait_send()
        else:
            copy.wait_recv()
        return carry

    lax.fori_loop(1, count, one, 0)


class Exchange:
    def __init__(self, axis, count, me, source, landing, sems):
        self.args = (axis, count, me, source, landing, sems[0], sems[1])

    def start(self):
        send_all(*self.args)

    def wait_recv(self):
        wait_all(*self.args, False)

    def wait_send(self):
        wait_all(*self.args, True)


def fold_lanes(value):
    half = value.shape[1] // 2
    return jnp.concatenate([value[:, :half], value[:, half:]], 0)


def unfold_lanes(value):
    half = value.shape[0] // 2
    return jnp.concatenate([value[:half], value[half:]], 1)


def views(refs, first, count, lanes):
    first = pl.multiple_of(first, count)
    return [ref.at[pl.ds(first, count), lanes] for ref in refs]


def reduce_start(ex_low, ex_bc, low_slots, bc_slots, low, bc, me):
    ex_low.start()
    ex_bc.start()
    low_slots[me] = low[me]
    bc_slots[me] = bc[me]


def reduce_middle(ex, low_slots, bc_slots, low_all, bc_all, me, count):
    ex[0].wait_recv()
    ex[1].wait_recv()

    def add(k, total):
        return (total[0] + low_slots[k].astype(F32), total[1] + bc_slots[k])

    zero = (jnp.zeros(low_slots.shape[1:], F32), jnp.zeros(bc_slots.shape[1:], F32))
    low_sum, bc_sum = lax.fori_loop(0, count, add, zero)
    low_all[me] = low_sum.astype(BF16)
    bc_all[me] = bc_sum
    ex[2].start()
    ex[3].start()


def spread_rows(source, target):
    per = source.shape[1]
    for e in range(source.shape[0]):
        target[e * per : (e + 1) * per, :] = source[e]


def core_body(
    dp, expert,
    xin, zin, cot, conv_weight, conv_bias, proj_mine, dt_mine, dt_bias, a_log, d_skip,
    gate_out, gradx_out, proj_out, dtw_out, small_all,
    send_proj, send_extra, send_dt, send_edge, all_proj, all_extra, all_dt, front,
    low_part, bc_part, low_slots, bc_slots, low_all, bc_all,
    low_part2, bc_part2, low_slots2, bc_slots2, low_all2, bc_all2,
    parts, slots, found, incoming,
    dtw_part, dtw_slots, pw_part, pw_slots, small_part, small_slots, edge_grad, after,
    proj_wide, proj_full, dt_full, padded, grads, preact, xconv, pre, step, gy, gate_factor,
    u_rows, y_rows, b_rows, q_rows, fold_b, fold_c, bx, cx, bc_rows, begin, hist, adjoint, prevs,
    *sems,
):
    seqs, tokens, width = zin.shape
    states = a_log.shape[0]
    taps = conv_weight.shape[0]
    reach = taps - 1
    rows = seqs * tokens
    rank = dt_full.shape[0]
    part = dt_mine.shape[0]
    proj_rows = proj_mine.shape[0]
    me = lax.axis_index("dp")
    mine = lax.axis_index("expert")
    hail("dp", dp, me)
    hail("expert", expert, mine)

    pairs = iter(range(0, len(sems), 2))

    def next_pair():
        i = next(pairs)
        return (sems[i], sems[i + 1])

    def over_dp(source, landing):
        return Exchange("dp", dp, me, source, landing, next_pair())

    def over_expert(source, landing):
        return Exchange("expert", expert, mine, source, landing, next_pair())

    def reduction(low, bc, low_in, bc_in, low_out, bc_out):
        return (
            over_expert(lambda p: low.at[p], lambda d: low_in.at[d]),
            over_expert(lambda p: bc.at[p], lambda d: bc_in.at[d]),
            over_expert(lambda p: low_out.at[mine], lambda d: low_out.at[d]),
            over_expert(lambda p: bc_out.at[mine], lambda d: bc_out.at[d]),
        )

    ex_proj = over_dp(lambda p: send_proj, lambda d: all_proj.at[d])
    ex_extra = over_dp(lambda p: send_extra, lambda d: all_extra.at[d])
    ex_dt = over_dp(lambda p: send_dt, lambda d: all_dt.at[d])
    ex_one = reduction(low_part, bc_part, low_slots, bc_slots, low_all, bc_all)
    ex_two = reduction(low_part2, bc_part2, low_slots2, bc_slots2, low_all2, bc_all2)
    ex_parts = over_dp(lambda p: parts.at[p], lambda d: slots.at[d])
    ex_found = over_dp(lambda p: found.at[p], lambda d: incoming.at[d])
    ex_dtw = over_dp(lambda p: dtw_part.at[p], lambda d: dtw_slots.at[d])
    ex_pw = over_dp(lambda p: pw_part.at[p], lambda d: pw_slots.at[d])
    ex_small = over_dp(lambda p: small_part.at[p], lambda d: small_slots.at[d])
    ex_total = over_dp(lambda p: small_all.at[me], lambda d: small_all.at[d])

    def neighbour(source, target, distance):
        pair = next_pair()
        return pltpu.make_async_remote_copy(
            src_ref=source,
            dst_ref=target,
            send_sem=pair[0],
            recv_sem=pair[1],
            device_id={"dp": lax.rem(me + dp + distance, dp)},
            device_id_type=MESH,
        )

    halo = neighbour(send_edge, front, 1)
    halo_back = neighbour(edge_grad, after, -1)

    proj32 = proj_mine[...].astype(F32)
    send_proj[...] = fold_lanes(proj32[:part]).astype(BF16)
    send_extra[...] = proj32[part:]
    send_dt[...] = fold_lanes(dt_mine[...].astype(F32)).astype(BF16)
    send_edge[...] = jnp.concatenate(
        [xin[s, tokens - 16 :, :].astype(F32)[8:] for s in range(seqs)], 0
    ).astype(BF16)
    all_proj[me] = send_proj[...]
    all_extra[me] = send_extra[...]
    all_dt[me] = send_dt[...]
    for s in range(seqs):
        here = slice(s * tokens, (s + 1) * tokens)
        z = zin[s].astype(F32)
        g = cot[s].astype(F32)
        sig = lax.logistic(z)
        gy[here, :] = g * z * sig
        gate_factor[here, :] = g * sig * (1.0 + z * (1.0 - sig))
        padded[s, 8:, :] = xin[s].astype(F32)
    rate_all = -jnp.exp(a_log[...])
    pl.semaphore_wait(pltpu.get_barrier_semaphore(), dp + expert - 2)

    halo.start()
    ex_proj.start()
    ex_extra.start()
    ex_dt.start()

    halo.wait_recv()
    keep = jnp.where(me == 0, 0.0, 1.0).astype(F32)
    lead = front[...].astype(F32) * keep
    for s in range(seqs):
        padded[s, 8 - reach : 8, :] = lead[8 * s + 8 - reach : 8 * s + 8, :]
        value = conv_bias[...] + jnp.zeros((tokens, width), F32)
        for k in range(taps):
            first = 8 - reach + k
            value = value + conv_weight[k : k + 1, :] * padded[s, first : first + tokens, :]
        here = slice(s * tokens, (s + 1) * tokens)
        preact[here, :] = value
        xconv[here, :] = (value * lax.logistic(value)).astype(BF16)
    ex_proj.wait_recv()
    ex_extra.wait_recv()
    for i in range(dp):
        proj_wide[i * proj_rows : i * proj_rows + part, :] = unfold_lanes(all_proj[i].astype(F32))
        proj_wide[i * proj_rows + part : (i + 1) * proj_rows, :] = all_extra[i]
    proj_full[...] = proj_wide[...].astype(BF16)
    x_flat = xconv[...]
    bc = dot_nt(proj_full[rank:, :], x_flat)
    per = bc_part.shape[1]
    for e in range(expert):
        bc_part[e] = bc[e * per : (e + 1) * per, :]
    low_part[...] = dot_nt(x_flat, proj_full[0:rank, :]).reshape(low_part.shape).astype(BF16)
    reduce_start(ex_one[0], ex_one[1], low_slots, bc_slots, low_part, bc_part, mine)
    ex_dt.wait_recv()
    for i in range(0, dp, 2):
        pair = [unfold_lanes(all_dt[i + j].astype(F32)) for j in range(2)]
        dt_full[i * part : (i + 2) * part, :] = jnp.concatenate(pair, 0).astype(BF16)
    reduce_middle(ex_one, low_slots, bc_slots, low_all, bc_all, mine, expert)
    ex_one[3].wait_recv()
    spread_rows(bc_all, bc_rows)
    for r in range(rows):
        bx[r] = jnp.broadcast_to(bc_rows[0:states, r : r + 1], (states, LANES))
        cx[r] = jnp.broadcast_to(bc_rows[states : 2 * states, r : r + 1], (states, LANES))
    ex_one[2].wait_recv()
    low = low_all[...].reshape(rows, rank)
    pre_value = dot_nn(low, dt_full[...]) + dt_bias[...]
    pre[...] = pre_value
    step_value = jnp.maximum(pre_value, 0.0) + jnp.log1p(jnp.exp(-jnp.abs(pre_value)))
    step[...] = step_value
    u_rows[...] = step_value * xconv[...].astype(F32)

    for block in range(width // LANES):
        lanes = slice(block * LANES, (block + 1) * LANES)
        rate = rate_all[:, lanes]

        def alone(k, carried):
            ahead = list(carried[:seqs])
            behind = list(carried[seqs:])
            for s in range(seqs):
                first = s * tokens + k * 8
                last = s * tokens + tokens - (k + 1) * 8
                step_f, u_f = views((step, u_rows), first, 8, lanes)
                step_b, gy_b = views((step, gy), last, 8, lanes)
                for i in range(8):
                    now = jnp.exp(step_f[i : i + 1, :] * rate)
                    ahead[s] = now * ahead[s] + bx[first + i] * u_f[i : i + 1, :]
                    j = 7 - i
                    now = jnp.exp(step_b[j : j + 1, :] * rate)
                    behind[s] = now * (cx[last + j] * gy_b[j : j + 1, :] + behind[s])
            return tuple(ahead + behind)

        zero = jnp.zeros((states, LANES), F32)
        ends = lax.fori_loop(0, tokens // 8, alone, (zero,) * (2 * seqs))
        for s in range(seqs):
            total = jnp.sum(step[s * tokens : (s + 1) * tokens, lanes], axis=0, keepdims=True)
            passing = jnp.exp(rate * total)
            for n in range(states):
                parts[s * states + n, 0:1, lanes] = ends[s][n : n + 1, :]
                parts[s * states + n, 1:2, lanes] = ends[seqs + s][n : n + 1, :]
                parts[s * states + n, 2:3, lanes] = passing[n : n + 1, :]

    ex_parts.start()
    slots[me] = parts[me]
    span = CHUNK * states
    turns = tokens // CHUNK
    spread = (
        (lax.broadcasted_iota(jnp.int32, (states, span), 1) & (states - 1))
        == lax.broadcasted_iota(jnp.int32, (states, span), 0)
    ).astype(F32)
    spread_half = spread.astype(BF16)
    own = (
        lax.shift_right_logical(
            lax.broadcasted_iota(jnp.int32, (rows, span), 1), states.bit_length() - 1
        )
        == (lax.broadcasted_iota(jnp.int32, (rows, span), 0) & (CHUNK - 1))
    ).astype(F32)
    across = jnp.transpose(bc_rows[...])
    b_diag = (dot_nn(across[:, :states].astype(BF16), spread_half) * own).astype(BF16)
    c_diag = (dot_nn(across[:, states:].astype(BF16), spread_half) * own).astype(BF16)
    own = own[:CHUNK]
    fold = own.astype(BF16)
    ex_parts.wait_recv()

    def prefix(k, carried):
        ahead, behind = carried
        late = dp - 1 - k
        found[k, 0:1, :] = ahead
        found[late, 1:2, :] = behind
        ahead = slots[k, 2:3, :] * ahead + slots[k, 0:1, :]
        behind = slots[late, 2:3, :] * behind + slots[late, 1:2, :]
        return (ahead, behind)

    zero = jnp.zeros((1, width), F32)
    lax.fori_loop(0, dp, prefix, (zero, zero))
    ex_found.start()
    incoming[me] = found[me]
    gy_half = gy[...].astype(BF16)
    u_half = u_rows[...].astype(BF16)
    ex_found.wait_recv()
    for s in range(seqs):
        for n in range(states):
            begin[s, n : n + 1, :] = incoming[s * states + n, 0:1, :]
            begin[seqs + s, n : n + 1, :] = incoming[s * states + n, 1:2, :]
        hist[s, 0] = begin[s].astype(BF16)

    rate_sums = []
    for block in range(width // LANES):
        lanes = slice(block * LANES, (block + 1) * LANES)
        rate = rate_all[:, lanes]

        def forward(k, carried):
            carried = list(carried)
            t = k * CHUNK
            for s in range(seqs):
                step_v, u_v = views((step, u_rows), s * tokens + t, CHUNK, lanes)
                for i in range(CHUNK):
                    now = jnp.exp(step_v[i : i + 1, :] * rate)
                    carried[s] = now * carried[s] + bx[s * tokens + t + i] * u_v[i : i + 1, :]
                    hist[s, t + i + 1, :, lanes] = carried[s].astype(BF16)
            return tuple(carried)

        lax.fori_loop(0, turns, forward, tuple(begin[s, :, lanes] for s in range(seqs)))

        def backward(k, carried):
            passed = list(carried[:seqs])
            rate_grad = list(carried[seqs:])
            first = tokens - (k + 1) * CHUNK
            for s in range(seqs):
                step_v, gy_v = views((step, gy), s * tokens + first, CHUNK, lanes)
                for i in reversed(range(CHUNK)):
                    t = first + i
                    step_row = step_v[i : i + 1, :]
                    now = jnp.exp(step_row * rate)
                    adj = cx[s * tokens + t] * gy_v[i : i + 1, :] + passed[s]
                    adjoint[s, t, :, lanes] = adj.astype(BF16)
                    passed[s] = now * adj
                    prev = passed[s] * hist[s, t, :, lanes].astype(F32) * rate
                    prevs[s, t, :, lanes] = prev.astype(BF16)
                    rate_grad[s] = rate_grad[s] + prev * step_row
            return tuple(passed + rate_grad)

        ends = lax.fori_loop(
            0,
            turns,
            backward,
            tuple(begin[seqs + s, :, lanes] for s in range(seqs))
            + (jnp.zeros((states, LANES), F32),) * seqs,
        )
        rate_sums.append(sum(ends[seqs + 1 :], ends[seqs]))

    for s in range(seqs):
        for k in range(turns):
            t = k * CHUNK
            here = slice(s * tokens + t, s * tokens + t + CHUNK)
            history = hist[s, t + 1 : t + 1 + CHUNK].reshape(span, width)
            y_rows[here, :] = dot_nn(c_diag[here], history)
            fold_c[here, :] = dot_nt(gy_half[here], history) * own
            adj = adjoint[s, t : t + CHUNK].reshape(span, width)
            b_rows[here, :] = dot_nn(b_diag[here], adj)
            fold_b[here, :] = dot_nt(u_half[here], adj) * own
            q_rows[here, :] = dot_nn(fold, prevs[s, t : t + CHUNK].reshape(span, width))

    exact = lax.Precision.HIGHEST
    grad_b = dot_nt(spread, fold_b[...], exact)
    grad_c = dot_nt(spread, fold_c[...], exact)
    grad_bc = jnp.concatenate([grad_b, grad_c], 0)
    for e in range(expert):
        bc_part2[e] = grad_bc[e * per : (e + 1) * per, :]
    x = xconv[...].astype(F32)
    b_adjoint = b_rows[...]
    grad_pre = (x * b_adjoint + q_rows[...]) * lax.logistic(pre[...])
    grad_round = grad_pre.astype(BF16)
    low_part2[...] = dot_nt(grad_round, dt_full[...]).reshape(low_part.shape).astype(BF16)
    reduce_start(ex_two[0], ex_two[1], low_slots2, bc_slots2, low_part2, bc_part2, mine)

    dtw = dot_tn(low_all[...].reshape(rows, rank), grad_round)
    for i in range(dp):
        dtw_part[i] = fold_lanes(dtw[i * part : (i + 1) * part]).astype(BF16)
    ex_dtw.start()
    dtw_slots[me] = dtw_part[me]
    sums = [jnp.concatenate(rate_sums, 1)]
    sums.append(jnp.sum(grad_pre, axis=0, keepdims=True))
    sums.append(jnp.sum(gy[...] * x, axis=0, keepdims=True))
    y_value = y_rows[...] + d_skip[...] * x
    gate_out[...] = (y_value * gate_factor[...]).astype(BF16).reshape(gate_out.shape)
    b_rows[...] = d_skip[...] * gy[...] + step[...] * b_adjoint
    reduce_middle(ex_two, low_slots2, bc_slots2, low_all2, bc_all2, mine, expert)
    ex_two[2].wait_recv()
    ex_two[3].wait_recv()

    spread_rows(bc_all2, bc_rows)
    low2 = low_all2[...].reshape(rows, rank)
    x_flat = xconv[...]
    pw = dot_tn(low2, x_flat)
    for i in range(dp):
        pw_part[i] = fold_lanes(pw[i * part : (i + 1) * part]).astype(BF16)
    ex_pw.start()
    pw_slots[me] = pw_part[me]
    state_terms = dot_nn(bc_rows[...].astype(BF16), x_flat)
    across = jnp.transpose(bc_rows[...]).astype(BF16)
    grad_conv = (
        b_rows[...] + dot_nn(low2, proj_full[0:rank, :]) + dot_nn(across, proj_full[rank:, :])
    )
    value = preact[...]
    sig = lax.logistic(value)
    grad_pre = grad_conv * sig * (1.0 + value * (1.0 - sig))
    conv_terms = [jnp.zeros((1, width), F32) for k in range(taps)]
    for s in range(seqs):
        part_grad = grad_pre[s * tokens : (s + 1) * tokens]
        grads[s, 0:tokens, :] = part_grad
        edge_grad[8 * s : 8 * s + 8, :] = part_grad[0:8]
        for k in range(taps):
            first = 8 - reach + k
            conv_terms[k] = conv_terms[k] + jnp.sum(
                part_grad * padded[s, first : first + tokens, :], axis=0, keepdims=True
            )
    halo_back.start()
    pieces = [state_terms[i : i + 1] for i in range(2 * states)]
    pieces += conv_terms
    pieces.append(jnp.sum(grad_pre, axis=0, keepdims=True))
    pieces += [sums[0][i : i + 1] for i in range(states)]
    pieces += sums[1:]
    while len(pieces) < 2 * dp:
        pieces.append(jnp.zeros((1, width), F32))
    for i, piece in enumerate(pieces):
        small_part[i // 2, i % 2 : i % 2 + 1, :] = piece
    ex_small.start()
    small_slots[me] = small_part[me]

    def add_slots(refs):
        def add(k, total):
            return tuple(t + ref[k].astype(F32) for t, ref in zip(total, refs))

        return lax.fori_loop(0, dp, add, tuple(jnp.zeros(ref.shape[1:], F32) for ref in refs))

    ex_dtw.wait_recv()
    dtw_out[...] = unfold_lanes(add_slots((dtw_slots,))[0])
    halo_back.wait_recv()
    keep = jnp.where(me == dp - 1, 0.0, 1.0).astype(F32)
    for s in range(seqs):
        grads[s, tokens:, :] = after[8 * s : 8 * s + 8, :] * keep
        result = jnp.zeros((tokens, width), F32)
        for k in range(taps):
            late = reach - k
            result = result + conv_weight[k : k + 1, :] * grads[s, late : late + tokens, :]
        gradx_out[s] = result.astype(BF16)
    ex_small.wait_recv()
    small_all[me] = add_slots((small_slots,))[0]
    ex_total.start()
    ex_pw.wait_recv()
    proj_out[...] = unfold_lanes(add_slots((pw_slots,))[0])
    for ex in (ex_proj, ex_extra, ex_dt) + ex_one + ex_two + (ex_parts, ex_found, ex_dtw):
        ex.wait_send()
    halo.wait_send()
    halo_back.wait_send()
    ex_pw.wait_send()
    ex_small.wait_send()
    ex_total.wait_recv()
    ex_total.wait_send()


def output_body(
    states2, taps, gate, gradx, proj, dtw, small,
    gradx_out, gate_out, proj_out, state_out, dtw_out, weight_out, bias_out, dtb_out, alog_out, skip_out,
):
    gradx_out[...] = gradx[...]
    gate_out[...] = gate[...]
    proj_out[...] = proj[...]
    dtw_out[...] = dtw[...]
    states = states2 // 2
    targets = [(state_out, i) for i in range(states2)]
    targets += [(weight_out, i) for i in range(taps)]
    targets.append((bias_out, 0))
    targets += [(alog_out, i) for i in range(states)]
    targets += [(dtb_out, 0), (skip_out, 0)]
    for i, (target, row) in enumerate(targets):
        target[row : row + 1, :] = small[i // 2, i % 2 : i % 2 + 1, :]


def body(
    xin, zin, cotangent, conv_weight, conv_bias, proj_weight, dt_weight, dt_bias, a_log, d_skip
):
    dp = lax.axis_size("dp")
    expert = lax.axis_size("expert")
    seqs, tokens, width = xin.shape
    taps = conv_weight.shape[0]
    states = a_log.shape[0]
    rows = seqs * tokens
    part = dt_weight.shape[0]
    proj_rows = proj_weight.shape[0]
    rank = part * dp
    half = width // 2

    low_shape = (expert, rows // expert, rank)
    bc_shape = (expert, 2 * states // expert, rows)
    flat = (rows, width)
    cube = (seqs, tokens, width)
    fold = (2 * part, half)
    extra = (proj_rows - part, width)

    def f32(*shape):
        return pltpu.VMEM(shape, F32)

    def bf16(*shape):
        return pltpu.VMEM(shape, BF16)

    reduction = [bf16(*low_shape), f32(*bc_shape)] * 3
    scratch = [bf16(*fold), f32(*extra), bf16(*fold), bf16(8 * seqs, width)]
    scratch += [bf16(dp, *fold), f32(dp, *extra), bf16(dp, *fold), bf16(8 * seqs, width)]
    scratch += reduction + reduction
    scratch += [f32(dp, 3, width), f32(dp, 3, width), f32(dp, 2, width), f32(dp, 2, width)]
    scratch += [bf16(dp, *fold)] * 4 + [f32(dp, 2, width)] * 2 + [f32(8 * seqs, width)] * 2
    scratch += [f32(proj_rows * dp, width), bf16(proj_rows * dp, width), bf16(rank, width)]
    scratch += [f32(seqs, tokens + 8, width)] * 2
    scratch += [f32(*flat), bf16(*flat), f32(*flat), f32(*flat), f32(*flat), f32(*flat)]
    scratch += [f32(*flat)] * 4 + [f32(rows, CHUNK * states)] * 2
    scratch += [f32(rows, states, LANES)] * 2
    scratch += [f32(2 * states, rows), f32(2 * seqs, states, width)]
    scratch += [bf16(seqs, tokens + 1, states, width)] + [bf16(seqs, tokens, states, width)] * 2
    order = [dp] * 3 + [expert] * 8 + [dp] * 6
    for count in order:
        scratch += [pltpu.SemaphoreType.DMA((count,))] * 2
    scratch += [pltpu.SemaphoreType.DMA] * 4

    gate, gradx, proj, dtw, small = pl.pallas_call(
        functools.partial(core_body, dp, expert),
        out_shape=(
            sds(cube, BF16),
            sds(cube, BF16),
            sds((part, width), F32),
            sds((part, width), F32),
            sds((dp, 2, width), F32),
        ),
        in_specs=[whole] * 10,
        out_specs=(whole,) * 5,
        scratch_shapes=scratch,
        compiler_params=pltpu.CompilerParams(
            collective_id=1, has_side_effects=True, vmem_limit_bytes=VMEM_BYTES
        ),
        name="core",
    )(
        xin,
        zin,
        cotangent,
        conv_weight,
        conv_bias[None, :],
        proj_weight,
        dt_weight,
        dt_bias[None, :],
        a_log,
        d_skip[None, :],
    )
    row = sds((1, width), F32)
    results = pl.pallas_call(
        functools.partial(output_body, 2 * states, taps),
        out_shape=(
            sds(cube, BF16),
            sds(cube, BF16),
            sds((part, width), F32),
            sds((2 * states, width), F32),
            sds((part, width), F32),
            sds((taps, width), F32),
            row,
            row,
            sds((states, width), F32),
            row,
        ),
        in_specs=[whole] * 5,
        out_specs=(whole,) * 10,
        compiler_params=pltpu.CompilerParams(vmem_limit_bytes=VMEM_BYTES),
        name="outputs",
    )(gate, gradx, proj, dtw, small)
    results = list(results)
    for i in (6, 7, 9):
        results[i] = results[i].reshape(width)
    return tuple(results)


def solution(mesh):
    return jax.shard_map(
        body,
        mesh=mesh,
        in_specs=(
            P(None, "dp", "expert"),
            P(None, "dp", "expert"),
            P(None, "dp", "expert"),
            P(None, "expert"),
            P("expert"),
            P("dp", "expert"),
            P("dp", "expert"),
            P("expert"),
            P(None, "expert"),
            P("expert"),
        ),
        out_specs=(
            P(None, "dp", "expert"),
            P(None, "dp", "expert"),
            P("dp", "expert"),
            P(None, "expert"),
            P("dp", "expert"),
            P(None, "expert"),
            P("expert"),
            P("expert"),
            P(None, "expert"),
            P("expert"),
        ),
        check_vma=False,
    )
```

time: 1580 us -> 122 us (0.08)
  waiting for transfers between devices: 734 us -> 0 us
  blocking collectives: 269 us -> 0 us
  local copies, waits for them, and re-layouts: 257 us -> 0 us
  other arithmetic: 232 us -> 0 us
  Pallas kernels: 0 us -> 120 us
  loops' own time: 49.1 us -> 0 us
    reduce_scatter x2 -> x0, waiting for transfers between devices: 444 us -> none  [the longest x1 222 us: body(): lax.psum_scatter(contract_first(dt_low, grad_dt_round), 'dp', scatter_dim...]
    psum x2 -> x0, blocking collectives: 191 us -> none  [the longest x1 141 us: body(): lax.psum((proj_terms[low_rank:], conv_terms, jnp.sum(grad_preact, axis=(0...]
    psum x2 -> x0, waiting for transfers between devices: 154 us -> none  [the longest x1 131 us: body(): projected = lax.psum(contract_last(x_flat, proj_full), 'expert')]
    reduce_sum x164 -> x0, other arithmetic: 139 us -> none  [the longest x64 69.3 us: one_turn(): jnp.sum(prev_term * decay_rate[None], axis=1)]
    all_gather x3 -> x0, waiting for transfers between devices: 136 us -> none  [prefix(): gathered = jax.tree.map(lambda a: lax.all_gather(a, axis), part)]
    pallas_call x0 -> x2, Pallas kernels: none -> 120 us  [the longest x1 118 us: body(): pl.pallas_call(functools.partial(core_body, dp, expert), out_shape=(sds(c...]
    mul x112 -> x0, local copies, waits for them, and re-layouts: 105 us -> none  [the longest x32 43.5 us: one_turn(): adjoint = c_part[:, offset, :, None] * gy_part[:, offset, None, :] + passed]
    all_gather x2 -> x0, blocking collectives: 77.6 us -> none  [the longest x1 43 us: body(): lax.all_gather(proj_weight, 'dp', axis=0, tiled=True)]
  transfers between devices with their start and end apart: 9 -> 0, of which waited for: 6 -> 0; matrix products, arithmetic and copies ran while one was open for 7% -> 0% of each run, Pallas kernels for 0% -> 0%
where the time goes in v2:
time: 122 us; the launch traced here: 121 us
  Pallas kernels  120 us (98%)
    pallas_call x1, Pallas kernels, body(): pl.pallas_call(functools.partial(core_body, dp, expert), out_shape=(sds(c...  118 us

profile of v2, /device:TPU:1, one launch (start us, length us, event | category | flops | bytes accessed | tf_op | source)
XLA Modules:
  0.0 120.7 jit_solution(764632874500211796)
XLA Ops:
  0.6 118.1 %core.1 = (bf16[2,128,512]{2,1,0:T(8,128)(2,1)}, bf16[2,128,512]{2,1,0:T(8,128)(2,1)}, f32[8,512]{1,0:T(8,128)}, f32[8,512]{1,0:T(8,128)}, f32[32,2,512]{2,1,0:T(2,128)}) custom-call(bf16[2,128,512]{2,1,0:T(8,128)(2,1)} %xin.1, bf16[2,128,512]{2,1,0:T(8,128)(2,1)} %zin.1, bf16[2,128,512]{2,1,0:T(8,128)(2,1)} %cot.1, f32[4,512]{1,0:T(4,128)} %conv_weight.1, ...), custom_call_target="tpu_custom_call" | custom-call | tf_op jit(solution)/shard_map/core/pallas_call | solution.py:577
  118.8 2.0 %outputs.1 = (bf16[2,128,512]{2,1,0:T(8,128)(2,1)}, bf16[2,128,512]{2,1,0:T(8,128)(2,1)}, f32[8,512]{1,0:T(8,128)}, f32[32,512]{1,0:T(8,128)}, f32[8,512]{1,0:T(...) custom-call(bf16[2,128,512]{2,1,0:T(8,128)(2,1)} %get-tuple-element., ...), custom_call_target="tpu_custom_call" | custom-call | tf_op jit(solution)/shard_map/outputs/pallas_call | solution.py:606

commit v3 on v2

--- a/solution.py
+++ b/solution.py
@@ -90,6 +90,18 @@
     def start(self):
         send_all(*self.args)
 
+    def start_one(self, peer):
+        axis, count, me, source, landing, send_sem, recv_sem = self.args
+        k = lax.rem(peer - me + count, count)
+        pltpu.make_async_remote_copy(
+            src_ref=source(peer),
+            dst_ref=landing(me),
+            send_sem=send_sem.at[k],
+            recv_sem=recv_sem.at[k],
+            device_id={axis: peer},
+            device_id_type=MESH,
+        ).start()
+
     def wait_recv(self):
         wait_all(*self.args, False)
 
@@ -146,11 +158,12 @@
     gate_out, gradx_out, proj_out, dtw_out, small_all,
     send_proj, send_extra, send_dt, send_edge, all_proj, all_extra, all_dt, front,
     low_part, bc_part, low_slots, bc_slots, low_all, bc_all,
-    low_part2, bc_part2, low_slots2, bc_slots2, low_all2, bc_all2,
+    part2, slots2, all2,
     parts, slots, found, incoming,
     dtw_part, dtw_slots, pw_part, pw_slots, small_part, small_slots, edge_grad, after,
     proj_wide, proj_full, dt_full, padded, grads, preact, xconv, pre, step, gy, gate_factor,
-    u_rows, y_rows, b_rows, q_rows, fold_b, fold_c, bx, cx, bc_rows, begin, hist, adjoint, prevs,
+    u_rows, y_rows, b_rows, g_rows, u_half, gy_half, g_half, b_diag, c_diag,
+    bx, cx, bc_rows, begin, hist, adjoint, prevs, decays, b_in, c_in,
     *sems,
 ):
     seqs, tokens, width = zin.shape
@@ -190,7 +203,8 @@
     ex_extra = over_dp(lambda p: send_extra, lambda d: all_extra.at[d])
     ex_dt = over_dp(lambda p: send_dt, lambda d: all_dt.at[d])
     ex_one = reduction(low_part, bc_part, low_slots, bc_slots, low_all, bc_all)
-    ex_two = reduction(low_part2, bc_part2, low_slots2, bc_slots2, low_all2, bc_all2)
+    ex_two = over_expert(lambda p: part2.at[p], lambda d: slots2.at[d])
+    ex_three = over_expert(lambda p: all2.at[mine], lambda d: all2.at[d])
     ex_parts = over_dp(lambda p: parts.at[p], lambda d: slots.at[d])
     ex_found = over_dp(lambda p: found.at[p], lambda d: incoming.at[d])
     ex_dtw = over_dp(lambda p: dtw_part.at[p], lambda d: dtw_slots.at[d])
@@ -255,9 +269,11 @@
     for i in range(dp):
         proj_wide[i * proj_rows : i * proj_rows + part, :] = unfold_lanes(all_proj[i].astype(F32))
         proj_wide[i * proj_rows + part : (i + 1) * proj_rows, :] = all_extra[i]
-    proj_full[...] = proj_wide[...].astype(BF16)
+    total = rank + 2 * states
+    proj_full[0:total, :] = proj_wide[...].astype(BF16)
+    proj_full[total:, :] = jnp.zeros((proj_full.shape[0] - total, width), BF16)
     x_flat = xconv[...]
-    bc = dot_nt(proj_full[rank:, :], x_flat)
+    bc = dot_nt(proj_full[rank:total, :], x_flat)
     per = bc_part.shape[1]
     for e in range(expert):
         bc_part[e] = bc[e * per : (e + 1) * per, :]
@@ -281,8 +297,13 @@
     step[...] = step_value
     u_rows[...] = step_value * xconv[...].astype(F32)
 
-    for block in range(width // LANES):
-        lanes = slice(block * LANES, (block + 1) * LANES)
+    wide = 2 * LANES
+
+    def across_lanes(tile, count):
+        return jnp.concatenate([tile] * count, 1)
+
+    for block in range(width // wide):
+        lanes = slice(block * wide, (block + 1) * wide)
         rate = rate_all[:, lanes]
 
         def alone(k, carried):
@@ -295,13 +316,15 @@
                 step_b, gy_b = views((step, gy), last, 8, lanes)
                 for i in range(8):
                     now = jnp.exp(step_f[i : i + 1, :] * rate)
-                    ahead[s] = now * ahead[s] + bx[first + i] * u_f[i : i + 1, :]
+                    b_tile = across_lanes(bx[first + i], 2)
+                    ahead[s] = now * ahead[s] + b_tile * u_f[i : i + 1, :]
                     j = 7 - i
                     now = jnp.exp(step_b[j : j + 1, :] * rate)
-                    behind[s] = now * (cx[last + j] * gy_b[j : j + 1, :] + behind[s])
+                    c_tile = across_lanes(cx[last + j], 2)
+                    behind[s] = now * (c_tile * gy_b[j : j + 1, :] + behind[s])
             return tuple(ahead + behind)
 
-        zero = jnp.zeros((states, LANES), F32)
+        zero = jnp.zeros((states, wide), F32)
         ends = lax.fori_loop(0, tokens // 8, alone, (zero,) * (2 * seqs))
         for s in range(seqs):
             total = jnp.sum(step[s * tokens : (s + 1) * tokens, lanes], axis=0, keepdims=True)
@@ -327,10 +350,26 @@
         == (lax.broadcasted_iota(jnp.int32, (rows, span), 0) & (CHUNK - 1))
     ).astype(F32)
     across = jnp.transpose(bc_rows[...])
-    b_diag = (dot_nn(across[:, :states].astype(BF16), spread_half) * own).astype(BF16)
-    c_diag = (dot_nn(across[:, states:].astype(BF16), spread_half) * own).astype(BF16)
+    b_diag[...] = (dot_nn(across[:, :states].astype(BF16), spread_half) * own).astype(BF16)
+    c_diag[...] = (dot_nn(across[:, states:].astype(BF16), spread_half) * own).astype(BF16)
     own = own[:CHUNK]
     fold = own.astype(BF16)
+    lanes_row = lax.broadcasted_iota(jnp.int32, (LANES, 2 * span), 0)
+    lanes_col = lax.broadcasted_iota(jnp.int32, (LANES, 2 * span), 1)
+    target = (lanes_col & (states - 1)) + jnp.where(lanes_col < span, 0, states)
+    gather_bc = (lanes_row == target).astype(F32).astype(BF16)
+    u_half[...] = u_rows[...].astype(BF16)
+    gy_half[...] = gy[...].astype(BF16)
+
+    def prepare(k, carry):
+        step_v, u_v = views((step, u_rows), k * 8, 8, slice(0, width))
+        for i in range(8):
+            r = k * 8 + i
+            decays[r] = jnp.exp(step_v[i : i + 1, :] * rate_all)
+            b_in[r] = across_lanes(bx[r], width // LANES) * u_v[i : i + 1, :]
+        return carry
+
+    lax.fori_loop(0, rows // 8, prepare, 0)
     ex_parts.wait_recv()
 
     def prefix(k, carried):
@@ -346,8 +385,15 @@
     lax.fori_loop(0, dp, prefix, (zero, zero))
     ex_found.start()
     incoming[me] = found[me]
-    gy_half = gy[...].astype(BF16)
-    u_half = u_rows[...].astype(BF16)
+
+    def prepare_back(k, carry):
+        gy_v = views((gy,), k * 8, 8, slice(0, width))[0]
+        for i in range(8):
+            r = k * 8 + i
+            c_in[r] = across_lanes(cx[r], width // LANES) * gy_v[i : i + 1, :]
+        return carry
+
+    lax.fori_loop(0, rows // 8, prepare_back, 0)
     ex_found.wait_recv()
     for s in range(seqs):
         for n in range(states):
@@ -355,104 +401,108 @@
             begin[seqs + s, n : n + 1, :] = incoming[s * states + n, 1:2, :]
         hist[s, 0] = begin[s].astype(BF16)
 
-    rate_sums = []
-    for block in range(width // LANES):
-        lanes = slice(block * LANES, (block + 1) * LANES)
-        rate = rate_all[:, lanes]
-
-        def forward(k, carried):
-            carried = list(carried)
-            t = k * CHUNK
-            for s in range(seqs):
-                step_v, u_v = views((step, u_rows), s * tokens + t, CHUNK, lanes)
-                for i in range(CHUNK):
-                    now = jnp.exp(step_v[i : i + 1, :] * rate)
-                    carried[s] = now * carried[s] + bx[s * tokens + t + i] * u_v[i : i + 1, :]
-                    hist[s, t + i + 1, :, lanes] = carried[s].astype(BF16)
-            return tuple(carried)
-
-        lax.fori_loop(0, turns, forward, tuple(begin[s, :, lanes] for s in range(seqs)))
-
-        def backward(k, carried):
-            passed = list(carried[:seqs])
-            rate_grad = list(carried[seqs:])
-            first = tokens - (k + 1) * CHUNK
-            for s in range(seqs):
-                step_v, gy_v = views((step, gy), s * tokens + first, CHUNK, lanes)
-                for i in reversed(range(CHUNK)):
-                    t = first + i
-                    step_row = step_v[i : i + 1, :]
-                    now = jnp.exp(step_row * rate)
-                    adj = cx[s * tokens + t] * gy_v[i : i + 1, :] + passed[s]
-                    adjoint[s, t, :, lanes] = adj.astype(BF16)
-                    passed[s] = now * adj
-                    prev = passed[s] * hist[s, t, :, lanes].astype(F32) * rate
-                    prevs[s, t, :, lanes] = prev.astype(BF16)
-                    rate_grad[s] = rate_grad[s] + prev * step_row
-            return tuple(passed + rate_grad)
-
-        ends = lax.fori_loop(
-            0,
-            turns,
-            backward,
-            tuple(begin[seqs + s, :, lanes] for s in range(seqs))
-            + (jnp.zeros((states, LANES), F32),) * seqs,
-        )
-        rate_sums.append(sum(ends[seqs + 1 :], ends[seqs]))
-
+    def forward(k, carried):
+        carried = list(carried)
+        for s in range(seqs):
+            for i in range(8):
+                t = k * 8 + i
+                carried[s] = decays[s * tokens + t] * carried[s] + b_in[s * tokens + t]
+                hist[s, t + 1] = carried[s].astype(BF16)
+        return tuple(carried)
+
+    lax.fori_loop(0, tokens // 8, forward, tuple(begin[s] for s in range(seqs)))
+
+    def backward(k, carried):
+        passed = list(carried[:seqs])
+        rate_grad = carried[seqs]
+        chunk = turns - 1 - k
+        first = chunk * CHUNK
+        folded = []
+        rounded = []
+        for s in range(seqs):
+            here = pl.ds(pl.multiple_of(s * tokens + first, CHUNK), CHUNK)
+            step_v = step.at[here, :]
+            for i in reversed(range(CHUNK)):
+                r = s * tokens + first + i
+                adj = c_in[r] + passed[s]
+                adjoint[s, i] = adj.astype(BF16)
+                passed[s] = decays[r] * adj
+                prev = passed[s] * hist[s, first + i].astype(F32) * rate_all
+                prevs[s, i] = prev.astype(BF16)
+                rate_grad = rate_grad + prev * step_v[i : i + 1, :]
+            history = hist[s, pl.ds(first + 1, CHUNK)].reshape(span, width)
+            adj = adjoint[s].reshape(span, width)
+            b_adjoint = dot_nn(b_diag[here, :], adj)
+            summed = dot_nn(fold, prevs[s].reshape(span, width))
+            grad_b = dot_nt(u_half[here, :], adj) * own
+            grad_c = dot_nt(gy_half[here, :], history) * own
+            folded.append(jnp.concatenate([grad_b, grad_c], 1))
+            x = xconv[here, :].astype(F32)
+            grad_pre = (x * b_adjoint + summed) * lax.logistic(pre[here, :])
+            g_rows[here, :] = grad_pre
+            rounded.append(grad_pre.astype(BF16))
+            g_half[here, :] = rounded[s]
+            b_rows[here, :] = d_skip[...] * gy[here, :] + step[here, :] * b_adjoint
+        folded = jnp.concatenate(folded, 0)
+        coarse = folded.astype(BF16)
+        fine = (folded - coarse.astype(F32)).astype(BF16)
+        halves = dot_nt(jnp.concatenate([coarse, fine], 0), gather_bc)
+        grad_bc = halves[: seqs * CHUNK] + halves[seqs * CHUNK :]
+        low_grad = dot_nt(jnp.concatenate(rounded, 0), dt_full[...])
+        message = jnp.concatenate([low_grad, grad_bc], 1).astype(BF16)
+        for s in range(seqs):
+            owner = s * turns + chunk
+            part2[owner] = message[s * CHUNK : (s + 1) * CHUNK]
+
+            @pl.when(mine != owner)
+            def _():
+                ex_two.start_one(owner)
+
+            @pl.when(mine == owner)
+            def _():
+                slots2[mine] = part2[mine]
+
+        return tuple(passed) + (rate_grad,)
+
+    ends = lax.fori_loop(
+        0,
+        turns,
+        backward,
+        tuple(begin[seqs + s] for s in range(seqs)) + (jnp.zeros((states, width), F32),),
+    )
+    rate_sum = ends[seqs]
+
+    dtw = dot_tn(low_all[...].reshape(rows, rank), g_half[...])
+    for i in range(dp):
+        dtw_part[i] = fold_lanes(dtw[i * part : (i + 1) * part]).astype(BF16)
+    ex_dtw.start()
+    dtw_slots[me] = dtw_part[me]
+    x = xconv[...].astype(F32)
+    sums = [rate_sum]
+    sums.append(jnp.sum(g_rows[...], axis=0, keepdims=True))
+    sums.append(jnp.sum(gy[...] * x, axis=0, keepdims=True))
+    ex_two.wait_recv()
+
+    def add_messages(k, total):
+        return total + slots2[k].astype(F32)
+
+    zero = jnp.zeros(slots2.shape[1:], F32)
+    all2[mine] = lax.fori_loop(0, expert, add_messages, zero).astype(BF16)
+    ex_three.start()
     for s in range(seqs):
         for k in range(turns):
             t = k * CHUNK
             here = slice(s * tokens + t, s * tokens + t + CHUNK)
             history = hist[s, t + 1 : t + 1 + CHUNK].reshape(span, width)
-            y_rows[here, :] = dot_nn(c_diag[here], history)
-            fold_c[here, :] = dot_nt(gy_half[here], history) * own
-            adj = adjoint[s, t : t + CHUNK].reshape(span, width)
-            b_rows[here, :] = dot_nn(b_diag[here], adj)
-            fold_b[here, :] = dot_nt(u_half[here], adj) * own
-            q_rows[here, :] = dot_nn(fold, prevs[s, t : t + CHUNK].reshape(span, width))
-
-    exact = lax.Precision.HIGHEST
-    grad_b = dot_nt(spread, fold_b[...], exact)
-    grad_c = dot_nt(spread, fold_c[...], exact)
-    grad_bc = jnp.concatenate([grad_b, grad_c], 0)
-    for e in range(expert):
-        bc_part2[e] = grad_bc[e * per : (e + 1) * per, :]
-    x = xconv[...].astype(F32)
-    b_adjoint = b_rows[...]
-    grad_pre = (x * b_adjoint + q_rows[...]) * lax.logistic(pre[...])
-    grad_round = grad_pre.astype(BF16)
-    low_part2[...] = dot_nt(grad_round, dt_full[...]).reshape(low_part.shape).astype(BF16)
-    reduce_start(ex_two[0], ex_two[1], low_slots2, bc_slots2, low_part2, bc_part2, mine)
-
-    dtw = dot_tn(low_all[...].reshape(rows, rank), grad_round)
-    for i in range(dp):
-        dtw_part[i] = fold_lanes(dtw[i * part : (i + 1) * part]).astype(BF16)
-    ex_dtw.start()
-    dtw_slots[me] = dtw_part[me]
-    sums = [jnp.concatenate(rate_sums, 1)]
-    sums.append(jnp.sum(grad_pre, axis=0, keepdims=True))
-    sums.append(jnp.sum(gy[...] * x, axis=0, keepdims=True))
+            y_rows[here, :] = dot_nn(c_diag[here, :], history)
     y_value = y_rows[...] + d_skip[...] * x
     gate_out[...] = (y_value * gate_factor[...]).astype(BF16).reshape(gate_out.shape)
-    b_rows[...] = d_skip[...] * gy[...] + step[...] * b_adjoint
-    reduce_middle(ex_two, low_slots2, bc_slots2, low_all2, bc_all2, mine, expert)
-    ex_two[2].wait_recv()
-    ex_two[3].wait_recv()
-
-    spread_rows(bc_all2, bc_rows)
-    low2 = low_all2[...].reshape(rows, rank)
+    ex_three.wait_recv()
+
+    grad_projected = all2[...].reshape(rows, all2.shape[2])
     x_flat = xconv[...]
-    pw = dot_tn(low2, x_flat)
-    for i in range(dp):
-        pw_part[i] = fold_lanes(pw[i * part : (i + 1) * part]).astype(BF16)
-    ex_pw.start()
-    pw_slots[me] = pw_part[me]
-    state_terms = dot_nn(bc_rows[...].astype(BF16), x_flat)
-    across = jnp.transpose(bc_rows[...]).astype(BF16)
-    grad_conv = (
-        b_rows[...] + dot_nn(low2, proj_full[0:rank, :]) + dot_nn(across, proj_full[rank:, :])
-    )
+    grad_conv = b_rows[...] + dot_nn(grad_projected, proj_full[...])
+    state_terms = dot_tn(grad_projected[:, rank:], x_flat)
     value = preact[...]
     sig = lax.logistic(value)
     grad_pre = grad_conv * sig * (1.0 + value * (1.0 - sig))
@@ -478,6 +528,11 @@
         small_part[i // 2, i % 2 : i % 2 + 1, :] = piece
     ex_small.start()
     small_slots[me] = small_part[me]
+    pw = dot_tn(grad_projected[:, :rank], x_flat)
+    for i in range(dp):
+        pw_part[i] = fold_lanes(pw[i * part : (i + 1) * part]).astype(BF16)
+    ex_pw.start()
+    pw_slots[me] = pw_part[me]
 
     def add_slots(refs):
         def add(k, total):
@@ -501,7 +556,7 @@
     ex_total.start()
     ex_pw.wait_recv()
     proj_out[...] = unfold_lanes(add_slots((pw_slots,))[0])
-    for ex in (ex_proj, ex_extra, ex_dt) + ex_one + ex_two + (ex_parts, ex_found, ex_dtw):
+    for ex in (ex_proj, ex_extra, ex_dt) + ex_one + (ex_two, ex_three, ex_parts, ex_found, ex_dtw):
         ex.wait_send()
     halo.wait_send()
     halo_back.wait_send()
@@ -559,17 +614,18 @@
     reduction = [bf16(*low_shape), f32(*bc_shape)] * 3
     scratch = [bf16(*fold), f32(*extra), bf16(*fold), bf16(8 * seqs, width)]
     scratch += [bf16(dp, *fold), f32(dp, *extra), bf16(dp, *fold), bf16(8 * seqs, width)]
-    scratch += reduction + reduction
+    scratch += reduction + [bf16(expert, rows // expert, rank + LANES)] * 3
     scratch += [f32(dp, 3, width), f32(dp, 3, width), f32(dp, 2, width), f32(dp, 2, width)]
     scratch += [bf16(dp, *fold)] * 4 + [f32(dp, 2, width)] * 2 + [f32(8 * seqs, width)] * 2
-    scratch += [f32(proj_rows * dp, width), bf16(proj_rows * dp, width), bf16(rank, width)]
+    scratch += [f32(proj_rows * dp, width), bf16(rank + LANES, width), bf16(rank, width)]
     scratch += [f32(seqs, tokens + 8, width)] * 2
     scratch += [f32(*flat), bf16(*flat), f32(*flat), f32(*flat), f32(*flat), f32(*flat)]
-    scratch += [f32(*flat)] * 4 + [f32(rows, CHUNK * states)] * 2
+    scratch += [f32(*flat)] * 4 + [bf16(*flat)] * 3 + [bf16(rows, CHUNK * states)] * 2
     scratch += [f32(rows, states, LANES)] * 2
     scratch += [f32(2 * states, rows), f32(2 * seqs, states, width)]
-    scratch += [bf16(seqs, tokens + 1, states, width)] + [bf16(seqs, tokens, states, width)] * 2
-    order = [dp] * 3 + [expert] * 8 + [dp] * 6
+    scratch += [bf16(seqs, tokens + 1, states, width)] + [bf16(seqs, CHUNK, states, width)] * 2
+    scratch += [f32(rows, states, width)] * 3
+    order = [dp] * 3 + [expert] * 6 + [dp] * 6
     for count in order:
         scratch += [pltpu.SemaphoreType.DMA((count,))] * 2
     scratch += [pltpu.SemaphoreType.DMA] * 4

time: 122 us -> 111 us (0.910)
  Pallas kernels: 120 us -> 110 us
    pallas_call x1, Pallas kernels: 118 us -> 108 us  [body(): pl.pallas_call(functools.partial(core_body, dp, expert), out_shape=(sds(c...]
where the time goes in v3:
time: 111 us
  Pallas kernels  110 us (99%)
    pallas_call x1, Pallas kernels, body(): pl.pallas_call(functools.partial(core_body, dp, expert), out_shape=(sds(c...  108 us

profile of v3, /device:TPU:1, one launch (start us, length us, event | category | flops | bytes accessed | tf_op | source)
XLA Modules:
  0.0 110.7 jit_solution(8119571966018060597)
XLA Ops:
  0.6 108.1 %core.1 = (bf16[2,128,512]{2,1,0:T(8,128)(2,1)}, bf16[2,128,512]{2,1,0:T(8,128)(2,1)}, f32[8,512]{1,0:T(8,128)}, f32[8,512]{1,0:T(8,128)}, f32[32,2,512]{2,1,0:T(2,128)}) custom-call(bf16[2,128,512]{2,1,0:T(8,128)(2,1)} %xin.1, bf16[2,128,512]{2,1,0:T(8,128)(2,1)} %zin.1, bf16[2,128,512]{2,1,0:T(8,128)(2,1)} %cot.1, f32[4,512]{1,0:T(4,128)} %conv_weight.1, ...), custom_call_target="tpu_custom_call" | custom-call | tf_op jit(solution)/shard_map/core/pallas_call | solution.py:633
  108.7 2.0 %outputs.1 = (bf16[2,128,512]{2,1,0:T(8,128)(2,1)}, bf16[2,128,512]{2,1,0:T(8,128)(2,1)}, f32[8,512]{1,0:T(8,128)}, f32[32,512]{1,0:T(8,128)}, f32[8,512]{1,0:T(...) custom-call(bf16[2,128,512]{2,1,0:T(8,128)(2,1)} %get-tuple-element., ...), custom_call_target="tpu_custom_call" | custom-call | tf_op jit(solution)/shard_map/outputs/pallas_call | solution.py:662

commit v4 on v3

--- a/solution.py
+++ b/solution.py
@@ -36,77 +36,41 @@
 
 def hail(axis, count, me):
     barrier = pltpu.get_barrier_semaphore()
-
-    def one(k, carry):
+    for k in range(1, count):
         pl.semaphore_signal(
             barrier, inc=1, device_id={axis: lax.rem(me + k, count)}, device_id_type=MESH
         )
-        return carry
-
-    lax.fori_loop(1, count, one, 0)
-
-
-def send_all(axis, count, me, source, landing, send_sem, recv_sem):
-    def one(k, carry):
-        peer = lax.rem(me + k, count)
+
+
+class Exchange:
+    def __init__(self, axis, count, me, source, landing, sems):
+        self.axis, self.count, self.me = axis, count, me
+        self.source, self.landing = source, landing
+        self.send_sem, self.recv_sem = sems
+
+    def start_one(self, peer):
         pltpu.make_async_remote_copy(
-            src_ref=source(peer),
-            dst_ref=landing(me),
-            send_sem=send_sem.at[k],
-            recv_sem=recv_sem.at[k],
-            device_id={axis: peer},
+            src_ref=self.source(peer),
+            dst_ref=self.landing.at[self.me],
+            send_sem=self.send_sem,
+            recv_sem=self.recv_sem,
+            device_id={self.axis: peer},
             device_id_type=MESH,
         ).start()
-        return carry
-
-    lax.fori_loop(1, count, one, 0)
-
-
-def wait_all(axis, count, me, source, landing, send_sem, recv_sem, sent):
-    def one(k, carry):
-        peer = lax.rem(me + k, count)
-        origin = lax.rem(me + count - k, count)
-        copy = pltpu.make_async_remote_copy(
-            src_ref=source(peer),
-            dst_ref=landing(origin),
-            send_sem=send_sem.at[k],
-            recv_sem=recv_sem.at[k],
-            device_id={axis: peer},
-            device_id_type=MESH,
-        )
-        if sent:
-            copy.wait_send()
-        else:
-            copy.wait_recv()
-        return carry
-
-    lax.fori_loop(1, count, one, 0)
-
-
-class Exchange:
-    def __init__(self, axis, count, me, source, landing, sems):
-        self.args = (axis, count, me, source, landing, sems[0], sems[1])
 
     def start(self):
-        send_all(*self.args)
-
-    def start_one(self, peer):
-        axis, count, me, source, landing, send_sem, recv_sem = self.args
-        k = lax.rem(peer - me + count, count)
-        pltpu.make_async_remote_copy(
-            src_ref=source(peer),
-            dst_ref=landing(me),
-            send_sem=send_sem.at[k],
-            recv_sem=recv_sem.at[k],
-            device_id={axis: peer},
-            device_id_type=MESH,
-        ).start()
+        for k in range(1, self.count):
+            self.start_one(lax.rem(self.me + k, self.count))
+
+    def wait_bytes(self, sem):
+        others = self.landing.at[pl.ds(0, self.count - 1)]
+        pltpu.make_async_copy(others, others, sem).wait()
 
     def wait_recv(self):
-        wait_all(*self.args, False)
+        self.wait_bytes(self.recv_sem)
 
     def wait_send(self):
-        wait_all(*self.args, True)
+        self.wait_bytes(self.send_sem)
 
 
 def fold_lanes(value):
@@ -193,24 +157,24 @@
 
     def reduction(low, bc, low_in, bc_in, low_out, bc_out):
         return (
-            over_expert(lambda p: low.at[p], lambda d: low_in.at[d]),
-            over_expert(lambda p: bc.at[p], lambda d: bc_in.at[d]),
-            over_expert(lambda p: low_out.at[mine], lambda d: low_out.at[d]),
-            over_expert(lambda p: bc_out.at[mine], lambda d: bc_out.at[d]),
+            over_expert(lambda p: low.at[p], low_in),
+            over_expert(lambda p: bc.at[p], bc_in),
+            over_expert(lambda p: low_out.at[mine], low_out),
+            over_expert(lambda p: bc_out.at[mine], bc_out),
         )
 
-    ex_proj = over_dp(lambda p: send_proj, lambda d: all_proj.at[d])
-    ex_extra = over_dp(lambda p: send_extra, lambda d: all_extra.at[d])
-    ex_dt = over_dp(lambda p: send_dt, lambda d: all_dt.at[d])
+    ex_proj = over_dp(lambda p: send_proj, all_proj)
+    ex_extra = over_dp(lambda p: send_extra, all_extra)
+    ex_dt = over_dp(lambda p: send_dt, all_dt)
     ex_one = reduction(low_part, bc_part, low_slots, bc_slots, low_all, bc_all)
-    ex_two = over_expert(lambda p: part2.at[p], lambda d: slots2.at[d])
-    ex_three = over_expert(lambda p: all2.at[mine], lambda d: all2.at[d])
-    ex_parts = over_dp(lambda p: parts.at[p], lambda d: slots.at[d])
-    ex_found = over_dp(lambda p: found.at[p], lambda d: incoming.at[d])
-    ex_dtw = over_dp(lambda p: dtw_part.at[p], lambda d: dtw_slots.at[d])
-    ex_pw = over_dp(lambda p: pw_part.at[p], lambda d: pw_slots.at[d])
-    ex_small = over_dp(lambda p: small_part.at[p], lambda d: small_slots.at[d])
-    ex_total = over_dp(lambda p: small_all.at[me], lambda d: small_all.at[d])
+    ex_two = over_expert(lambda p: part2.at[p], slots2)
+    ex_three = over_expert(lambda p: all2.at[mine], all2)
+    ex_parts = over_dp(lambda p: parts.at[p], slots)
+    ex_found = over_dp(lambda p: found.at[p], incoming)
+    ex_dtw = over_dp(lambda p: dtw_part.at[p], dtw_slots)
+    ex_pw = over_dp(lambda p: pw_part.at[p], pw_slots)
+    ex_small = over_dp(lambda p: small_part.at[p], small_slots)
+    ex_total = over_dp(lambda p: small_all.at[me], small_all)
 
     def neighbour(source, target, distance):
         pair = next_pair()
@@ -625,10 +589,7 @@
     scratch += [f32(2 * states, rows), f32(2 * seqs, states, width)]
     scratch += [bf16(seqs, tokens + 1, states, width)] + [bf16(seqs, CHUNK, states, width)] * 2
     scratch += [f32(rows, states, width)] * 3
-    order = [dp] * 3 + [expert] * 6 + [dp] * 6
-    for count in order:
-        scratch += [pltpu.SemaphoreType.DMA((count,))] * 2
-    scratch += [pltpu.SemaphoreType.DMA] * 4
+    scratch += [pltpu.SemaphoreType.DMA] * 34
 
     gate, gradx, proj, dtw, small = pl.pallas_call(
         functools.partial(core_body, dp, expert),

time: 111 us -> 104 us (0.937)
  Pallas kernels: 110 us -> 103 us
    pallas_call x1, Pallas kernels: 108 us -> 101 us  [body(): pl.pallas_call(functools.partial(core_body, dp, expert), out_shape=(sds(c...]
where the time goes in v4:
time: 104 us; the launch traced here: 103 us
  Pallas kernels  103 us (99%)
    pallas_call x1, Pallas kernels, body(): pl.pallas_call(functools.partial(core_body, dp, expert), out_shape=(sds(c...  101 us

profile of v4, /device:TPU:1, one launch (start us, length us, event | category | flops | bytes accessed | tf_op | source)
XLA Modules:
  0.0 103.3 jit_solution(16283513139227056346)
XLA Ops:
  0.6 100.7 %core.1 = (bf16[2,128,512]{2,1,0:T(8,128)(2,1)}, bf16[2,128,512]{2,1,0:T(8,128)(2,1)}, f32[8,512]{1,0:T(8,128)}, f32[8,512]{1,0:T(8,128)}, f32[32,2,512]{2,1,0:T(2,128)}) custom-call(bf16[2,128,512]{2,1,0:T(8,128)(2,1)} %xin.1, bf16[2,128,512]{2,1,0:T(8,128)(2,1)} %zin.1, bf16[2,128,512]{2,1,0:T(8,128)(2,1)} %cot.1, f32[4,512]{1,0:T(4,128)} %conv_weight.1, ...), custom_call_target="tpu_custom_call" | custom-call | tf_op jit(solution)/shard_map/core/pallas_call | solution.py:594
  101.4 2.0 %outputs.1 = (bf16[2,128,512]{2,1,0:T(8,128)(2,1)}, bf16[2,128,512]{2,1,0:T(8,128)(2,1)}, f32[8,512]{1,0:T(8,128)}, f32[32,512]{1,0:T(8,128)}, f32[8,512]{1,0:T(...) custom-call(bf16[2,128,512]{2,1,0:T(8,128)(2,1)} %get-tuple-element., ...), custom_call_target="tpu_custom_call" | custom-call | tf_op jit(solution)/shard_map/outputs/pallas_call | solution.py:623

commit v5 on v4

--- a/solution.py
+++ b/solution.py
@@ -34,12 +34,21 @@
     return lax.dot_general(left, right, (((0,), (0,)), ((), ())), preferred_element_type=F32)
 
 
-def hail(axis, count, me):
+TORUS = {"dp": (4, 8), "expert": (8, 2)}
+
+
+def partners(axis, me):
+    outer, inner = TORUS[axis]
+    steps = [(a, b) for a in range(outer) for b in range(inner) if a + b > 0]
+    steps.sort(key=lambda step: -min(step[0], outer - step[0]) - min(step[1], inner - step[1]))
+    here, there = me // inner, lax.rem(me, inner)
+    return [lax.rem(here + a, outer) * inner + lax.rem(there + b, inner) for a, b in steps]
+
+
+def hail(axis, me):
     barrier = pltpu.get_barrier_semaphore()
-    for k in range(1, count):
-        pl.semaphore_signal(
-            barrier, inc=1, device_id={axis: lax.rem(me + k, count)}, device_id_type=MESH
-        )
+    for peer in partners(axis, me):
+        pl.semaphore_signal(barrier, inc=1, device_id={axis: peer}, device_id_type=MESH)
 
 
 class Exchange:
@@ -59,8 +68,8 @@
         ).start()
 
     def start(self):
-        for k in range(1, self.count):
-            self.start_one(lax.rem(self.me + k, self.count))
+        for peer in partners(self.axis, self.me):
+            self.start_one(peer)
 
     def wait_bytes(self, sem):
         others = self.landing.at[pl.ds(0, self.count - 1)]
@@ -140,8 +149,8 @@
     proj_rows = proj_mine.shape[0]
     me = lax.axis_index("dp")
     mine = lax.axis_index("expert")
-    hail("dp", dp, me)
-    hail("expert", expert, mine)
+    hail("dp", me)
+    hail("expert", mine)
 
     pairs = iter(range(0, len(sems), 2))
 
@@ -271,25 +280,31 @@
         rate = rate_all[:, lanes]
 
         def alone(k, carried):
-            ahead = list(carried[:seqs])
-            behind = list(carried[seqs:])
+            ahead = list(carried)
             for s in range(seqs):
                 first = s * tokens + k * 8
-                last = s * tokens + tokens - (k + 1) * 8
                 step_f, u_f = views((step, u_rows), first, 8, lanes)
-                step_b, gy_b = views((step, gy), last, 8, lanes)
                 for i in range(8):
                     now = jnp.exp(step_f[i : i + 1, :] * rate)
+                    decays[first + i, :, lanes] = now
                     b_tile = across_lanes(bx[first + i], 2)
                     ahead[s] = now * ahead[s] + b_tile * u_f[i : i + 1, :]
-                    j = 7 - i
-                    now = jnp.exp(step_b[j : j + 1, :] * rate)
+            return tuple(ahead)
+
+        def alone_back(k, carried):
+            behind = list(carried)
+            for s in range(seqs):
+                last = s * tokens + tokens - (k + 1) * 8
+                gy_b = views((gy,), last, 8, lanes)[0]
+                for j in reversed(range(8)):
+                    now = decays[last + j, :, lanes]
                     c_tile = across_lanes(cx[last + j], 2)
                     behind[s] = now * (c_tile * gy_b[j : j + 1, :] + behind[s])
-            return tuple(ahead + behind)
+            return tuple(behind)
 
         zero = jnp.zeros((states, wide), F32)
-        ends = lax.fori_loop(0, tokens // 8, alone, (zero,) * (2 * seqs))
+        ends = lax.fori_loop(0, tokens // 8, alone, (zero,) * seqs)
+        ends = ends + lax.fori_loop(0, tokens // 8, alone_back, (zero,) * seqs)
         for s in range(seqs):
             total = jnp.sum(step[s * tokens : (s + 1) * tokens, lanes], axis=0, keepdims=True)
             passing = jnp.exp(rate * total)
@@ -326,10 +341,9 @@
     gy_half[...] = gy[...].astype(BF16)
 
     def prepare(k, carry):
-        step_v, u_v = views((step, u_rows), k * 8, 8, slice(0, width))
+        u_v = views((u_rows,), k * 8, 8, slice(0, width))[0]
         for i in range(8):
             r = k * 8 + i
-            decays[r] = jnp.exp(step_v[i : i + 1, :] * rate_all)
             b_in[r] = across_lanes(bx[r], width // LANES) * u_v[i : i + 1, :]
         return carry
 

time: 104 us -> 98.5 us (0.947)
  Pallas kernels: 103 us -> 97.5 us
    pallas_call x1, Pallas kernels: 101 us -> 95.5 us  [body(): pl.pallas_call(functools.partial(core_body, dp, expert), out_shape=(sds(c...]
where the time goes in v5:
time: 98.5 us; the launch traced here: 98.1 us
  Pallas kernels  97.5 us (99%)
    pallas_call x1, Pallas kernels, body(): pl.pallas_call(functools.partial(core_body, dp, expert), out_shape=(sds(c...  95.5 us

profile of v5, /device:TPU:1, one launch (start us, length us, event | category | flops | bytes accessed | tf_op | source)
XLA Modules:
  0.0 98.1 jit_solution(5999932211650225176)
XLA Ops:
  0.6 95.5 %core.1 = (bf16[2,128,512]{2,1,0:T(8,128)(2,1)}, bf16[2,128,512]{2,1,0:T(8,128)(2,1)}, f32[8,512]{1,0:T(8,128)}, f32[8,512]{1,0:T(8,128)}, f32[32,2,512]{2,1,0:T(2,128)}) custom-call(bf16[2,128,512]{2,1,0:T(8,128)(2,1)} %xin.1, bf16[2,128,512]{2,1,0:T(8,128)(2,1)} %zin.1, bf16[2,128,512]{2,1,0:T(8,128)(2,1)} %cot.1, f32[4,512]{1,0:T(4,128)} %conv_weight.1, ...), custom_call_target="tpu_custom_call" | custom-call | tf_op jit(solution)/shard_map/core/pallas_call | solution.py:608
  96.2 2.0 %outputs.1 = (bf16[2,128,512]{2,1,0:T(8,128)(2,1)}, bf16[2,128,512]{2,1,0:T(8,128)(2,1)}, f32[8,512]{1,0:T(8,128)}, f32[32,512]{1,0:T(8,128)}, f32[8,512]{1,0:T(...) custom-call(bf16[2,128,512]{2,1,0:T(8,128)(2,1)} %get-tuple-element., ...), custom_call_target="tpu_custom_call" | custom-call | tf_op jit(solution)/shard_map/outputs/pallas_call | solution.py:637

commit v6 on v5

--- a/solution.py
+++ b/solution.py
@@ -97,9 +97,8 @@
     return [ref.at[pl.ds(first, count), lanes] for ref in refs]
 
 
-def reduce_start(ex_low, ex_bc, low_slots, bc_slots, low, bc, me):
+def reduce_start(ex_low, low_slots, bc_slots, low, bc, me):
     ex_low.start()
-    ex_bc.start()
     low_slots[me] = low[me]
     bc_slots[me] = bc[me]
 
@@ -112,11 +111,11 @@
         return (total[0] + low_slots[k].astype(F32), total[1] + bc_slots[k])
 
     zero = (jnp.zeros(low_slots.shape[1:], F32), jnp.zeros(bc_slots.shape[1:], F32))
-    low_sum, bc_sum = lax.fori_loop(0, count, add, zero)
+    low_sum, bc_sum = lax.fori_loop(0, count, add, zero, unroll=8)
     low_all[me] = low_sum.astype(BF16)
     bc_all[me] = bc_sum
+    ex[3].start()
     ex[2].start()
-    ex[3].start()
 
 
 def spread_rows(source, target):
@@ -221,9 +220,8 @@
     pl.semaphore_wait(pltpu.get_barrier_semaphore(), dp + expert - 2)
 
     halo.start()
+    ex_extra.start()
     ex_proj.start()
-    ex_extra.start()
-    ex_dt.start()
 
     halo.wait_recv()
     keep = jnp.where(me == 0, 0.0, 1.0).astype(F32)
@@ -250,19 +248,21 @@
     per = bc_part.shape[1]
     for e in range(expert):
         bc_part[e] = bc[e * per : (e + 1) * per, :]
+    ex_one[1].start()
     low_part[...] = dot_nt(x_flat, proj_full[0:rank, :]).reshape(low_part.shape).astype(BF16)
-    reduce_start(ex_one[0], ex_one[1], low_slots, bc_slots, low_part, bc_part, mine)
+    reduce_start(ex_one[0], low_slots, bc_slots, low_part, bc_part, mine)
+    ex_dt.start()
+    reduce_middle(ex_one, low_slots, bc_slots, low_all, bc_all, mine, expert)
     ex_dt.wait_recv()
     for i in range(0, dp, 2):
         pair = [unfold_lanes(all_dt[i + j].astype(F32)) for j in range(2)]
         dt_full[i * part : (i + 2) * part, :] = jnp.concatenate(pair, 0).astype(BF16)
-    reduce_middle(ex_one, low_slots, bc_slots, low_all, bc_all, mine, expert)
     ex_one[3].wait_recv()
+    ex_one[2].wait_recv()
     spread_rows(bc_all, bc_rows)
     for r in range(rows):
         bx[r] = jnp.broadcast_to(bc_rows[0:states, r : r + 1], (states, LANES))
         cx[r] = jnp.broadcast_to(bc_rows[states : 2 * states, r : r + 1], (states, LANES))
-    ex_one[2].wait_recv()
     low = low_all[...].reshape(rows, rank)
     pre_value = dot_nn(low, dt_full[...]) + dt_bias[...]
     pre[...] = pre_value
@@ -270,7 +270,7 @@
     step[...] = step_value
     u_rows[...] = step_value * xconv[...].astype(F32)
 
-    wide = 2 * LANES
+    wide = width
 
     def across_lanes(tile, count):
         return jnp.concatenate([tile] * count, 1)
@@ -287,7 +287,7 @@
                 for i in range(8):
                     now = jnp.exp(step_f[i : i + 1, :] * rate)
                     decays[first + i, :, lanes] = now
-                    b_tile = across_lanes(bx[first + i], 2)
+                    b_tile = across_lanes(bx[first + i], wide // LANES)
                     ahead[s] = now * ahead[s] + b_tile * u_f[i : i + 1, :]
             return tuple(ahead)
 
@@ -298,7 +298,7 @@
                 gy_b = views((gy,), last, 8, lanes)[0]
                 for j in reversed(range(8)):
                     now = decays[last + j, :, lanes]
-                    c_tile = across_lanes(cx[last + j], 2)
+                    c_tile = across_lanes(cx[last + j], wide // LANES)
                     behind[s] = now * (c_tile * gy_b[j : j + 1, :] + behind[s])
             return tuple(behind)
 
@@ -360,7 +360,7 @@
         return (ahead, behind)
 
     zero = jnp.zeros((1, width), F32)
-    lax.fori_loop(0, dp, prefix, (zero, zero))
+    lax.fori_loop(0, dp, prefix, (zero, zero), unroll=8)
     ex_found.start()
     incoming[me] = found[me]
 
@@ -465,7 +465,7 @@
         return total + slots2[k].astype(F32)
 
     zero = jnp.zeros(slots2.shape[1:], F32)
-    all2[mine] = lax.fori_loop(0, expert, add_messages, zero).astype(BF16)
+    all2[mine] = lax.fori_loop(0, expert, add_messages, zero, unroll=8).astype(BF16)
     ex_three.start()
     for s in range(seqs):
         for k in range(turns):
@@ -489,12 +489,14 @@
         part_grad = grad_pre[s * tokens : (s + 1) * tokens]
         grads[s, 0:tokens, :] = part_grad
         edge_grad[8 * s : 8 * s + 8, :] = part_grad[0:8]
+    halo_back.start()
+    for s in range(seqs):
+        part_grad = grad_pre[s * tokens : (s + 1) * tokens]
         for k in range(taps):
             first = 8 - reach + k
             conv_terms[k] = conv_terms[k] + jnp.sum(
                 part_grad * padded[s, first : first + tokens, :], axis=0, keepdims=True
             )
-    halo_back.start()
     pieces = [state_terms[i : i + 1] for i in range(2 * states)]
     pieces += conv_terms
     pieces.append(jnp.sum(grad_pre, axis=0, keepdims=True))
@@ -516,7 +518,8 @@
         def add(k, total):
             return tuple(t + ref[k].astype(F32) for t, ref in zip(total, refs))
 
-        return lax.fori_loop(0, dp, add, tuple(jnp.zeros(ref.shape[1:], F32) for ref in refs))
+        zeros = tuple(jnp.zeros(ref.shape[1:], F32) for ref in refs)
+        return lax.fori_loop(0, dp, add, zeros, unroll=8)
 
     ex_dtw.wait_recv()
     dtw_out[...] = unfold_lanes(add_slots((dtw_slots,))[0])

time: 98.5 us -> 94.6 us (0.960)
  Pallas kernels: 97.5 us -> 93.8 us
    pallas_call x1, Pallas kernels: 95.5 us -> 91.8 us  [body(): pl.pallas_call(functools.partial(core_body, dp, expert), out_shape=(sds(c...]
where the time goes in v6:
time: 94.6 us; the launch traced here: 94.4 us
  Pallas kernels  93.8 us (99%)
    pallas_call x1, Pallas kernels, body(): pl.pallas_call(functools.partial(core_body, dp, expert), out_shape=(sds(c...  91.8 us
    pallas_call x1, Pallas kernels, body(): pl.pallas_call(functools.partial(output_body, 2 * states, taps), out_shap...  1.95 us

profile of v6, /device:TPU:1, one launch (start us, length us, event | category | flops | bytes accessed | tf_op | source)
XLA Modules:
  0.0 94.4 jit_solution(21568216887465146)
XLA Ops:
  0.6 91.8 %core.1 = (bf16[2,128,512]{2,1,0:T(8,128)(2,1)}, bf16[2,128,512]{2,1,0:T(8,128)(2,1)}, f32[8,512]{1,0:T(8,128)}, f32[8,512]{1,0:T(8,128)}, f32[32,2,512]{2,1,0:T(2,128)}) custom-call(bf16[2,128,512]{2,1,0:T(8,128)(2,1)} %xin.1, bf16[2,128,512]{2,1,0:T(8,128)(2,1)} %zin.1, bf16[2,128,512]{2,1,0:T(8,128)(2,1)} %cot.1, f32[4,512]{1,0:T(4,128)} %conv_weight.1, ...), custom_call_target="tpu_custom_call" | custom-call | tf_op jit(solution)/shard_map/core/pallas_call | solution.py:611
  92.5 2.0 %outputs.1 = (bf16[2,128,512]{2,1,0:T(8,128)(2,1)}, bf16[2,128,512]{2,1,0:T(8,128)(2,1)}, f32[8,512]{1,0:T(8,128)}, f32[32,512]{1,0:T(8,128)}, f32[8,512]{1,0:T(...) custom-call(bf16[2,128,512]{2,1,0:T(8,128)(2,1)} %get-tuple-element., ...), custom_call_target="tpu_custom_call" | custom-call | tf_op jit(solution)/shard_map/outputs/pallas_call | solution.py:640
